TPU v7x, 32 devices: a whole 2x2x4 slice. The times are simulated.
32 devices in a mesh: gz: 16 (over z, x, core), gy: 2 (over y).
Axes of the slice: x: 2, y: 2, z: 4, core: 2. Of those that a mesh axis runs over, the one named last changes fastest.
Arguments:
- saved_order_parameter: float32 [128, 32, 512], P('gz', 'gy'), may hold values from 0 to 1
- saved_heat_level: float32 [128, 32, 512], P('gz', 'gy'), may hold values from 0 to 1.5
- kinetic_rate_field: float32 [128, 32, 512], P('gz', 'gy'), may hold values from 0.5 to 2
- order_parameter_adjoint_seed: float32 [128, 32, 512], P('gz', 'gy'), may hold values from -6 to 6
- heat_level_adjoint_seed: float32 [128, 32, 512], P('gz', 'gy'), may hold values from -6 to 6
Outputs:
- start_phase: float32 [128, 32, 512], P('gz', 'gy')
- start_temp: float32 [128, 32, 512], P('gz', 'gy')
- grad_mobility: float32 [128, 32, 512], P('gz', 'gy')
All inputs are finite; a program needn't handle non-finite values.
Results may differ from a plain program's by a relative error of at most 0.00002.
Values sent between devices are 32-bit elements; how exact they have to be, the bound alone decides.
A program may use at most 64 MiB of HBM per device.

v0:
```python
import jax
import jax.numpy as jnp
from jax import lax
from jax.sharding import PartitionSpec as P

TIME_STEP = 0.15
ENERGY_SCALE = 0.5
ANISOTROPY = 0.05
GRAD_FLOOR = 0.01
LATENT_HEAT = 1.8
DRIVE_SCALE = 0.9
DRIVE_SHARP = 10.0
MELT_POINT = 1.0


def from_behind(block, axis, distance):
    devices = range(lax.axis_size(axis))
    route = [(i - distance, i) for i in devices if i - distance in devices]
    return lax.ppermute(block, axis, route)


def extended(cells, sides, width):
    for axis, dim in sides:
        count = lax.axis_size(axis)
        ends = count - 1
        head = lax.slice_in_dim(cells, 0, width, axis=dim)
        tail = lax.slice_in_dim(cells, cells.shape[dim] - width, cells.shape[dim], axis=dim)
        cells = jnp.concatenate(
            [
                lax.ppermute(tail, axis, [(i, (i + 1) % count) for i in range(ends)]),
                cells,
                lax.ppermute(head, axis, [((i + 1) % count, i) for i in range(ends)]),
            ],
            axis=dim,
        )
    return cells


def advance_solver_step(phase_wide, temp_wide, kinetic_rate_field):
    padded = jnp.pad(phase_wide, ((0, 0), (0, 0), (2, 2)))
    grad_z = 0.5 * (padded[2:, 1:-1, 1:-1] - padded[:-2, 1:-1, 1:-1])
    grad_y = 0.5 * (padded[1:-1, 2:, 1:-1] - padded[1:-1, :-2, 1:-1])
    grad_x = 0.5 * (padded[1:-1, 1:-1, 2:] - padded[1:-1, 1:-1, :-2])
    sq_z = grad_z * grad_z
    sq_y = grad_y * grad_y
    sq_x = grad_x * grad_x
    squared = sq_z + sq_y + sq_x + GRAD_FLOOR
    quartic = (sq_z * sq_z + sq_y * sq_y + sq_x * sq_x) / (squared * squared)
    anisotropy = 1.0 + ANISOTROPY * (4.0 * quartic - 3.0)
    aniso_sq = anisotropy * anisotropy
    factor_a = 16.0 * ANISOTROPY * anisotropy / squared
    flux_z = ENERGY_SCALE * (aniso_sq * grad_z + factor_a * grad_z * (sq_z - quartic * squared))
    flux_y = ENERGY_SCALE * (aniso_sq * grad_y + factor_a * grad_y * (sq_y - quartic * squared))
    flux_x = ENERGY_SCALE * (aniso_sq * grad_x + factor_a * grad_x * (sq_x - quartic * squared))
    divergence = 0.5 * (flux_z[2:, 1:-1, 1:-1] - flux_z[:-2, 1:-1, 1:-1])
    divergence = divergence + 0.5 * (flux_y[1:-1, 2:, 1:-1] - flux_y[1:-1, :-2, 1:-1])
    divergence = divergence + 0.5 * (flux_x[1:-1, 1:-1, 2:] - flux_x[1:-1, 1:-1, :-2])
    phase_now = phase_wide[2:-2, 2:-2]
    temp_now = temp_wide[2:-2, 2:-2]
    driving = DRIVE_SCALE / jnp.pi * jnp.arctan(DRIVE_SHARP * (MELT_POINT - temp_now))
    growth = kinetic_rate_field * (
        divergence + phase_now * (1.0 - phase_now) * (phase_now - 0.5 + driving)
    )
    new_phase = phase_now + TIME_STEP * growth
    temp_x = jnp.pad(temp_now, ((0, 0), (0, 0), (1, 1)))
    laplacian = (
        temp_wide[3:-1, 2:-2]
        + temp_wide[1:-3, 2:-2]
        + temp_wide[2:-2, 3:-1]
        + temp_wide[2:-2, 1:-3]
    )
    laplacian = laplacian + temp_x[:, :, 2:] + temp_x[:, :, :-2] - 6.0 * temp_now
    new_temp = temp_now + TIME_STEP * laplacian + LATENT_HEAT * (new_phase - phase_now)
    return (new_phase, new_temp)


def fold_rims(sensitivity_order_parameter, sensitivity_heat_level):
    stacked = jnp.stack((sensitivity_order_parameter, sensitivity_heat_level))
    lower_rim = stacked[:, :2]
    upper_rim = stacked[:, -2:]
    middle = stacked[:, 2:-2]
    from_above = from_behind(lower_rim, "gz", -1)
    from_below = from_behind(upper_rim, "gz", 1)
    middle = jnp.concatenate(
        (middle[:, :2] + from_below, middle[:, 2:-2], middle[:, -2:] + from_above), axis=1
    )
    lower_rim = middle[:, :, :2]
    upper_rim = middle[:, :, -2:]
    middle = middle[:, :, 2:-2]
    from_above = from_behind(lower_rim, "gy", -1)
    from_below = from_behind(upper_rim, "gy", 1)
    middle = jnp.concatenate(
        (middle[:, :, :2] + from_below, middle[:, :, 2:-2], middle[:, :, -2:] + from_above), axis=2
    )
    return (middle[0], middle[1])


def body(
    saved_order_parameter,
    saved_heat_level,
    kinetic_rate_field,
    order_parameter_adjoint_seed,
    heat_level_adjoint_seed,
):
    initial_extended = extended(
        jnp.stack((saved_order_parameter, saved_heat_level)), (("gz", 1), ("gy", 2)), 2
    )
    succeeding_order_parameter, succeeding_heat_level = advance_solver_step(
        initial_extended[0], initial_extended[1], kinetic_rate_field
    )
    state_wide = extended(
        jnp.stack((succeeding_order_parameter, succeeding_heat_level)), (("gz", 1), ("gy", 2)), 2
    )
    discarded_result, sensitivity_latest = jax.vjp(
        advance_solver_step, state_wide[0], state_wide[1], kinetic_rate_field
    )
    sensitivity_order_parameter, sensitivity_heat_level, latest_kinetic_rate = sensitivity_latest(
        (order_parameter_adjoint_seed, heat_level_adjoint_seed)
    )
    halfway_order_parameter, halfway_heat_level = fold_rims(
        sensitivity_order_parameter, sensitivity_heat_level
    )
    discarded_result, prior_backward_sweep = jax.vjp(
        advance_solver_step, initial_extended[0], initial_extended[1], kinetic_rate_field
    )
    sensitivity_order_parameter, sensitivity_heat_level, early_mob = prior_backward_sweep(
        (halfway_order_parameter, halfway_heat_level)
    )
    start_phase, start_temp = fold_rims(sensitivity_order_parameter, sensitivity_heat_level)
    return (start_phase, start_temp, latest_kinetic_rate + early_mob)


def solution(mesh):
    return jax.shard_map(
        body,
        mesh=mesh,
        in_specs=(
            P("gz", "gy", None),
            P("gz", "gy", None),
            P("gz", "gy", None),
            P("gz", "gy", None),
            P("gz", "gy", None),
        ),
        out_specs=(P("gz", "gy", None), P("gz", "gy", None), P("gz", "gy", None)),
        check_vma=False,
    )
```

profile of v0, /device:TPU:8, one launch (start us, length us, event | category | flops | bytes accessed | tf_op | source)
XLA Modules:
  0.0 103.5 jit_solution(4041236659130677262)
XLA Ops:
  0.7 1.0 pad_maximum_fusion.13
  1.7 1.9 %collective-permute-start = (f32[2,2,16,512]{3,2,1,0:T(8,128)S(1)}, f32[2,2,16,512]{3,2,1,0:T(8,128)S(1)}, u32[]{:S(2)}, u32[]{:S(2)}) collective-permute-start(f32[2,2,16,512]{3,2,1,0:T(8,128)S(1)} %get-tuple-element.80), channel_id=1, source_target_pairs={{0,2},{2,4},{4,6},{6,8},{8,10},{10,12},{12,14},{14,16},{16,18},{18... | collective-permute-start | bytes 393224 | tf_op jit(solution)/shard_map/ppermute | solution.py:30
  3.6 4.5 %collective-permute-start.1 = (f32[2,2,16,512]{3,2,1,0:T(8,128)S(1)}, f32[2,2,16,512]{3,2,1,0:T(8,128)S(1)}, u32[]{:S(2)}, u32[]{:S(2)}) collective-permute-start(f32[2,2,16,512]{3,2,1,0:T(8,128)S(1)} %get-tuple-element.81), channel_id=1, source_target_pairs={{2,0},{4,2},{6,4},{8,6},{10,8},{12,10},{14,12},{16,14},{18,16},{20... | collective-permute-start | bytes 393224 | tf_op jit(solution)/shard_map/ppermute | solution.py:32
  8.1 0.7 collective-permute-done
  8.9 1.8 %collective-permute-done.1 = f32[2,2,16,512]{3,2,1,0:T(8,128)S(1)} collective-permute-done((f32[2,2,16,512]{3,2,1,0:T(8,128)S(1)}, f32[2,2,16,512]{3,2,1,0:T(8,128)S(1)}, u32[]{:S(2)}, u32[]{:S(2)}) %collective-permute-start.1) | collective-permute-done | bytes 131104 | tf_op jit(solution)/shard_map/ppermute | solution.py:32
  10.6 1.2 %pad_maximum_fusion.21 = (f32[2,12,2,512]{3,2,1,0:T(2,128)S(1)}, f32[2,12,2,512]{3,2,1,0:T(2,128)S(1)}) fusion(f32[2,2,16,512]{3,2,1,0:T(8,128)S(1)} %collective-permute-done.1, f32[2,2,16,512]{3,2,1,0:T(8,128)S(1)} %collective-permute-done, f32[1,8,16,512]{3,2,1,0:T(8,128)} %bitcast.43, f32[1,8,16,512]{3,2,1,0:T(8,128)} %bitcast.46), kind=kLoop, calls=%fused_computation.221 | loop fusion | flops 147456 | bytes 983040 | tf_op jit(solution)/shard_map/slice | solution.py:27
  11.8 3.4 %collective-permute-start.2 = (f32[2,12,2,512]{3,2,1,0:T(2,128)S(1)}, f32[2,12,2,512]{3,2,1,0:T(2,128)S(1)}, u32[]{:S(2)}, u32[]{:S(2)}) collective-permute-start(f32[2,12,2,512]{3,2,1,0:T(2,128)S(1)} %get-tuple-element.70), channel_id=1, source_target_pairs={{0,1},{2,3},{4,5},{6,7},{8,9},{10,11},{12,13},{14,15},{16,17},{18,... | collective-permute-start | bytes 294920 | tf_op jit(solution)/shard_map/ppermute | solution.py:30
  15.3 1.3 %collective-permute-start.3 = (f32[2,12,2,512]{3,2,1,0:T(2,128)S(1)}, f32[2,12,2,512]{3,2,1,0:T(2,128)S(1)}, u32[]{:S(2)}, u32[]{:S(2)}) collective-permute-start(f32[2,12,2,512]{3,2,1,0:T(2,128)S(1)} %get-tuple-element.71), channel_id=1, source_target_pairs={{1,0},{3,2},{5,4},{7,6},{9,8},{11,10},{13,12},{15,14},{17,16},{19,... | collective-permute-start | bytes 294920 | tf_op jit(solution)/shard_map/ppermute | solution.py:32
  16.6 1.7 %collective-permute-done.2 = f32[2,12,2,512]{3,2,1,0:T(2,128)S(1)} collective-permute-done((f32[2,12,2,512]{3,2,1,0:T(2,128)S(1)}, f32[2,12,2,512]{3,2,1,0:T(2,128)S(1)}, u32[]{:S(2)}, u32[]{:S(2)}) %collective-permute-start.2) | collective-permute-done | bytes 98336 | tf_op jit(solution)/shard_map/ppermute | solution.py:30
  18.3 4.1 %collective-permute-done.3 = f32[2,12,2,512]{3,2,1,0:T(2,128)S(1)} collective-permute-done((f32[2,12,2,512]{3,2,1,0:T(2,128)S(1)}, f32[2,12,2,512]{3,2,1,0:T(2,128)S(1)}, u32[]{:S(2)}, u32[]{:S(2)}) %collective-permute-start.3) | collective-permute-done | bytes 98336 | tf_op jit(solution)/shard_map/ppermute | solution.py:32
  22.7 1.0 %add_multiply_fusion.11 = (f32[10,18,514]{2,1,0:T(8,128)S(1)}, f32[10,18,514]{2,1,0:T(8,128)S(1)}, f32[10,18,514]{2,1,0:T(8,128)S(1)}, f32[10,18,514]{2,1,0:T(8,...) fusion(f32[12,20,512]{2,1,0:T(8,128)S(1)} %get-tuple-element.60), kind=kLoop, calls=%fused_computation.98 | loop fusion | flops 3053160 | bytes 3082080 | tf_op jit(solution)/shard_map/mul | solution.py:52
  23.8 0.6 add_multiply_fusion.10
  24.7 0.7 fusion.79
  25.8 2.1 %collective-permute-start.4 = (f32[2,2,16,512]{3,2,1,0:T(8,128)S(1)}, f32[2,2,16,512]{3,2,1,0:T(8,128)S(1)}, u32[]{:S(2)}, u32[]{:S(2)}) collective-permute-start(f32[2,2,16,512]{3,2,1,0:T(8,128)S(1)} %get-tuple-element.78), channel_id=1, source_target_pairs={{0,2},{2,4},{4,6},{6,8},{8,10},{10,12},{12,14},{14,16},{16,18},{18... | collective-permute-start | bytes 393224 | tf_op jit(solution)/shard_map/ppermute | solution.py:30
  27.9 4.5 %collective-permute-start.5 = (f32[2,2,16,512]{3,2,1,0:T(8,128)S(1)}, f32[2,2,16,512]{3,2,1,0:T(8,128)S(1)}, u32[]{:S(2)}, u32[]{:S(2)}) collective-permute-start(f32[2,2,16,512]{3,2,1,0:T(8,128)S(1)} %get-tuple-element.79), channel_id=1, source_target_pairs={{2,0},{4,2},{6,4},{8,6},{10,8},{12,10},{14,12},{16,14},{18,16},{20... | collective-permute-start | bytes 393224 | tf_op jit(solution)/shard_map/ppermute | solution.py:32
  32.4 0.7 collective-permute-done.4
  33.1 1.8 %collective-permute-done.5 = f32[2,2,16,512]{3,2,1,0:T(8,128)S(1)} collective-permute-done((f32[2,2,16,512]{3,2,1,0:T(8,128)S(1)}, f32[2,2,16,512]{3,2,1,0:T(8,128)S(1)}, u32[]{:S(2)}, u32[]{:S(2)}) %collective-permute-start.5) | collective-permute-done | bytes 131104 | tf_op jit(solution)/shard_map/ppermute | solution.py:32
  35.0 1.5 %collective-permute-start.6 = (f32[2,12,2,512]{3,2,1,0:T(2,128)S(1)}, f32[2,12,2,512]{3,2,1,0:T(2,128)S(1)}, u32[]{:S(2)}, u32[]{:S(2)}) collective-permute-start(f32[2,12,2,512]{3,2,1,0:T(2,128)S(1)} %get-tuple-element.68), channel_id=1, source_target_pairs={{0,1},{2,3},{4,5},{6,7},{8,9},{10,11},{12,13},{14,15},{16,17},{18,... | collective-permute-start | bytes 294920 | tf_op jit(solution)/shard_map/ppermute | solution.py:30
  36.5 1.3 %collective-permute-start.7 = (f32[2,12,2,512]{3,2,1,0:T(2,128)S(1)}, f32[2,12,2,512]{3,2,1,0:T(2,128)S(1)}, u32[]{:S(2)}, u32[]{:S(2)}) collective-permute-start(f32[2,12,2,512]{3,2,1,0:T(2,128)S(1)} %get-tuple-element.69), channel_id=1, source_target_pairs={{1,0},{3,2},{5,4},{7,6},{9,8},{11,10},{13,12},{15,14},{17,16},{19,... | collective-permute-start | bytes 294920 | tf_op jit(solution)/shard_map/ppermute | solution.py:32
  37.8 0.8 collective-permute-done.6
  38.6 4.3 %collective-permute-done.7 = f32[2,12,2,512]{3,2,1,0:T(2,128)S(1)} collective-permute-done((f32[2,12,2,512]{3,2,1,0:T(2,128)S(1)}, f32[2,12,2,512]{3,2,1,0:T(2,128)S(1)}, u32[]{:S(2)}, u32[]{:S(2)}) %collective-permute-start.7) | collective-permute-done | bytes 98336 | tf_op jit(solution)/shard_map/ppermute | solution.py:32
  43.3 1.0 %add_multiply_fusion.2 = (f32[10,18,514]{2,1,0:T(8,128)S(1)}, f32[10,18,514]{2,1,0:T(8,128)S(1)}, f32[10,18,514]{2,1,0:T(8,128)S(1)}, f32[10,18,514]{2,1,0:T(8,128)S(1)}) fusion(f32[12,20,512]{2,1,0:T(8,128)S(1)} %get-tuple-element.58), kind=kLoop, calls=%fused_computation.80 | loop fusion | flops 3053160 | bytes 1971840 | tf_op jit(solution)/shard_map/jvp()/mul | solution.py:52
  44.3 0.7 fusion.55
  45.1 2.6 %fusion.91 = (f32[10,18,514]{2,1,0:T(8,128)S(1)}, f32[10,18,514]{2,1,0:T(8,128)S(1)}, f32[10,18,514]{2,1,0:T(8,128)S(1)}, f32[10,18,514]{2,1,0:T(8,128)S(1)}, f32[10,18,514]{2,1,0:T(8,128)S(1)}) fusion(f32[10,18,514]{2,1,0:T(8,128)S(1)} %get-tuple-element.6, f32[8,16,512]{2,1,0:T(8,128)S(1)} %get-tuple-element.67, f32[8,16,512]{2,1,0:T(8,128)S(1)} %get-tuple-element.66, ...), kind=kLoop, calls=%fused_computation.235 | loop fusion | flops 8604360 | bytes 3484928 | tf_op jit(solution)/shard_map/transpose(jvp())/neg | solution.py:43
  47.6 1.5 %fusion.93 = (f32[10,18,514]{2,1,0:T(8,128)S(1)}, f32[10,18,514]{2,1,0:T(8,128)S(1)}, f32[10,18,514]{2,1,0:T(8,128)S(1)}, f32[10,18,514]{2,1,0:T(8,128)S(1)}, f32[10,18,514]{2,1,0:T(8,128)S(1)}) fusion(f32[10,18,514]{2,1,0:T(8,128)S(1)} %get-tuple-element.7, f32[10,18,514]{2,1,0:T(8,128)S(1)} %get-tuple-element.22, ...), kind=kLoop, calls=%fused_computation.236 | loop fusion | flops 5643720 | bytes 4225088 | tf_op jit(solution)/shard_map/transpose(jvp())/neg | solution.py:42
  49.2 1.0 fusion.37
  50.2 1.9 %collective-permute-start.8 = (f32[2,2,20,512]{3,2,1,0:T(8,128)S(1)}, f32[2,2,20,512]{3,2,1,0:T(8,128)S(1)}, u32[]{:S(2)}, u32[]{:S(2)}) collective-permute-start(f32[2,2,20,512]{3,2,1,0:T(8,128)S(1)} %pad_maximum_fusion.9), channel_id=1, source_target_pairs={{0,2},{2,4},{4,6},{6,8},{8,10},{10,12},{12,14},{14,16},{16,18},{18... | collective-permute-start | bytes 491528 | tf_op jit(solution)/shard_map/ppermute | solution.py:19
  52.2 6.0 %collective-permute-done.8 = f32[2,2,20,512]{3,2,1,0:T(8,128)S(1)} collective-permute-done((f32[2,2,20,512]{3,2,1,0:T(8,128)S(1)}, f32[2,2,20,512]{3,2,1,0:T(8,128)S(1)}, u32[]{:S(2)}, u32[]{:S(2)}) %collective-permute-start.8) | collective-permute-done | bytes 163872 | tf_op jit(solution)/shard_map/ppermute | solution.py:19
  58.2 1.9 %collective-permute-start.9 = (f32[2,2,20,512]{3,2,1,0:T(8,128)S(1)}, f32[2,2,20,512]{3,2,1,0:T(8,128)S(1)}, u32[]{:S(2)}, u32[]{:S(2)}) collective-permute-start(f32[2,2,20,512]{3,2,1,0:T(8,128)S(1)} %get-tuple-element.57), channel_id=1, source_target_pairs={{2,0},{4,2},{6,4},{8,6},{10,8},{12,10},{14,12},{16,14},{18,16},{20... | collective-permute-start | bytes 491528 | tf_op jit(solution)/shard_map/ppermute | solution.py:19
  60.1 3.1 %collective-permute-done.9 = f32[2,2,20,512]{3,2,1,0:T(8,128)S(1)} collective-permute-done((f32[2,2,20,512]{3,2,1,0:T(8,128)S(1)}, f32[2,2,20,512]{3,2,1,0:T(8,128)S(1)}, u32[]{:S(2)}, u32[]{:S(2)}) %collective-permute-start.9) | collective-permute-done | bytes 163872 | tf_op jit(solution)/shard_map/ppermute | solution.py:19
  63.3 1.5 %collective-permute-start.10 = (f32[2,8,2,512]{3,2,1,0:T(2,128)S(1)}, f32[2,8,2,512]{3,2,1,0:T(2,128)S(1)}, u32[]{:S(2)}, u32[]{:S(2)}) collective-permute-start(f32[2,8,2,512]{3,2,1,0:T(2,128)S(1)} %pad_maximum_fusion.25), channel_id=1, source_target_pairs={{0,1},{2,3},{4,5},{6,7},{8,9},{10,11},{12,13},{14,15},{16,17},{18,... | collective-permute-start | bytes 196616 | tf_op jit(solution)/shard_map/ppermute | solution.py:19
  64.9 1.9 %collective-permute-done.10 = f32[2,8,2,512]{3,2,1,0:T(2,128)S(1)} collective-permute-done((f32[2,8,2,512]{3,2,1,0:T(2,128)S(1)}, f32[2,8,2,512]{3,2,1,0:T(2,128)S(1)}, u32[]{:S(2)}, u32[]{:S(2)}) %collective-permute-start.10) | collective-permute-done | bytes 65568 | tf_op jit(solution)/shard_map/ppermute | solution.py:19
  66.8 1.5 %collective-permute-start.11 = (f32[2,8,2,512]{3,2,1,0:T(2,128)S(1)}, f32[2,8,2,512]{3,2,1,0:T(2,128)S(1)}, u32[]{:S(2)}, u32[]{:S(2)}) collective-permute-start(f32[2,8,2,512]{3,2,1,0:T(2,128)S(1)} %get-tuple-element.65), channel_id=1, source_target_pairs={{1,0},{3,2},{5,4},{7,6},{9,8},{11,10},{13,12},{15,14},{17,16},{19,... | collective-permute-start | bytes 196616 | tf_op jit(solution)/shard_map/ppermute | solution.py:19
  68.4 4.5 %collective-permute-done.11 = f32[2,8,2,512]{3,2,1,0:T(2,128)S(1)} collective-permute-done((f32[2,8,2,512]{3,2,1,0:T(2,128)S(1)}, f32[2,8,2,512]{3,2,1,0:T(2,128)S(1)}, u32[]{:S(2)}, u32[]{:S(2)}) %collective-permute-start.11) | collective-permute-done | bytes 65568 | tf_op jit(solution)/shard_map/ppermute | solution.py:19
  73.1 1.5 %fusion.60 = (f32[8,16,512]{2,1,0:T(8,128)}, f32[8,16,512]{2,1,0:T(8,128)S(1)}, f32[8,16,512]{2,1,0:T(8,128)S(1)}) fusion(f32[10,18,514]{2,1,0:T(8,128)S(1)} %get-tuple-element.53, f32[10,18,514]{2,1,0:T(8,128)S(1)} %get-tuple-element.52, f32[10,18,514]{2,1,0:T(8,128)S(1)} %get-tuple-element.5, f32[8,16,512]{2,1,0:T(8,128)S(1)} %get-tuple-element.30, ...), kind=kLoop, calls=%fused_computation.160 | loop fusion | flops 1638400 | bytes 4194304 | tf_op jit(solution)/shard_map/add | solution.py:130
  74.6 0.7 fusion.53
  75.5 2.0 %fusion.84 = (f32[10,18,514]{2,1,0:T(8,128)S(1)}, f32[10,18,514]{2,1,0:T(8,128)S(1)}, f32[10,18,514]{2,1,0:T(8,128)S(1)}, f32[10,18,514]{2,1,0:T(8,128)S(1)}) fusion(f32[10,18,514]{2,1,0:T(8,128)S(1)} %get-tuple-element.37, f32[10,18,514]{2,1,0:T(8,128)S(1)} %get-tuple-element.47, f32[10,18,514]{2,1,0:T(8,128)S(1)} %get-tuple-element.33, ...), kind=kLoop, calls=%fused_computation.231 | loop fusion | flops 7771680 | bytes 4965248 | tf_op jit(solution)/shard_map/transpose(jvp())/neg | solution.py:43
  77.5 1.3 %fusion.86 = (f32[10,18,514]{2,1,0:T(8,128)S(1)}, f32[10,18,514]{2,1,0:T(8,128)S(1)}, f32[10,18,514]{2,1,0:T(8,128)S(1)}, f32[10,18,514]{2,1,0:T(8,128)S(1)}) fusion(f32[10,18,514]{2,1,0:T(8,128)S(1)} %get-tuple-element.36, f32[10,18,514]{2,1,0:T(8,128)S(1)} %get-tuple-element.12, f32[10,18,514]{2,1,0:T(8,128)S(1)} %get-tuple-element.11, ...), kind=kLoop, calls=%fused_computation.232 | loop fusion | flops 4440960 | bytes 5335328 | tf_op jit(solution)/shard_map/transpose(jvp())/neg | solution.py:42
  78.8 0.9 fusion.35
  79.8 1.9 %collective-permute-start.12 = (f32[2,2,20,512]{3,2,1,0:T(8,128)S(1)}, f32[2,2,20,512]{3,2,1,0:T(8,128)S(1)}, u32[]{:S(2)}, u32[]{:S(2)}) collective-permute-start(f32[2,2,20,512]{3,2,1,0:T(8,128)S(1)} %pad_maximum_fusion.7), channel_id=1, source_target_pairs={{0,2},{2,4},{4,6},{6,8},{8,10},{10,12},{12,14},{14,16},{16,18},{18... | collective-permute-start | bytes 491528 | tf_op jit(solution)/shard_map/ppermute | solution.py:19
  81.7 6.0 %collective-permute-done.12 = f32[2,2,20,512]{3,2,1,0:T(8,128)S(1)} collective-permute-done((f32[2,2,20,512]{3,2,1,0:T(8,128)S(1)}, f32[2,2,20,512]{3,2,1,0:T(8,128)S(1)}, u32[]{:S(2)}, u32[]{:S(2)}) %collective-permute-start.12) | collective-permute-done | bytes 163872 | tf_op jit(solution)/shard_map/ppermute | solution.py:19
  87.7 1.9 %collective-permute-start.13 = (f32[2,2,20,512]{3,2,1,0:T(8,128)S(1)}, f32[2,2,20,512]{3,2,1,0:T(8,128)S(1)}, u32[]{:S(2)}, u32[]{:S(2)}) collective-permute-start(f32[2,2,20,512]{3,2,1,0:T(8,128)S(1)} %get-tuple-element.55), channel_id=1, source_target_pairs={{2,0},{4,2},{6,4},{8,6},{10,8},{12,10},{14,12},{16,14},{18,16},{20... | collective-permute-start | bytes 491528 | tf_op jit(solution)/shard_map/ppermute | solution.py:19
  89.7 3.1 %collective-permute-done.13 = f32[2,2,20,512]{3,2,1,0:T(8,128)S(1)} collective-permute-done((f32[2,2,20,512]{3,2,1,0:T(8,128)S(1)}, f32[2,2,20,512]{3,2,1,0:T(8,128)S(1)}, u32[]{:S(2)}, u32[]{:S(2)}) %collective-permute-start.13) | collective-permute-done | bytes 163872 | tf_op jit(solution)/shard_map/ppermute | solution.py:19
  92.9 1.6 %collective-permute-start.14 = (f32[2,8,2,512]{3,2,1,0:T(2,128)S(1)}, f32[2,8,2,512]{3,2,1,0:T(2,128)S(1)}, u32[]{:S(2)}, u32[]{:S(2)}) collective-permute-start(f32[2,8,2,512]{3,2,1,0:T(2,128)S(1)} %pad_maximum_fusion.23), channel_id=1, source_target_pairs={{0,1},{2,3},{4,5},{6,7},{8,9},{10,11},{12,13},{14,15},{16,17},{18,... | collective-permute-start | bytes 196616 | tf_op jit(solution)/shard_map/ppermute | solution.py:19
  94.5 1.9 %collective-permute-done.14 = f32[2,8,2,512]{3,2,1,0:T(2,128)S(1)} collective-permute-done((f32[2,8,2,512]{3,2,1,0:T(2,128)S(1)}, f32[2,8,2,512]{3,2,1,0:T(2,128)S(1)}, u32[]{:S(2)}, u32[]{:S(2)}) %collective-permute-start.14) | collective-permute-done | bytes 65568 | tf_op jit(solution)/shard_map/ppermute | solution.py:19
  96.4 1.3 %collective-permute-start.15 = (f32[2,8,2,512]{3,2,1,0:T(2,128)S(1)}, f32[2,8,2,512]{3,2,1,0:T(2,128)S(1)}, u32[]{:S(2)}, u32[]{:S(2)}) collective-permute-start(f32[2,8,2,512]{3,2,1,0:T(2,128)S(1)} %get-tuple-element.63), channel_id=1, source_target_pairs={{1,0},{3,2},{5,4},{7,6},{9,8},{11,10},{13,12},{15,14},{17,16},{19,... | collective-permute-start | bytes 196616 | tf_op jit(solution)/shard_map/ppermute | solution.py:19
  97.8 4.7 %collective-permute-done.15 = f32[2,8,2,512]{3,2,1,0:T(2,128)S(1)} collective-permute-done((f32[2,8,2,512]{3,2,1,0:T(2,128)S(1)}, f32[2,8,2,512]{3,2,1,0:T(2,128)S(1)}, u32[]{:S(2)}, u32[]{:S(2)}) %collective-permute-start.15) | collective-permute-done | bytes 65568 | tf_op jit(solution)/shard_map/ppermute | solution.py:19
  102.7 0.8 slice_bitcast_fusion.4
  (39 shorter events, 2.6 us)
Async XLA Ops:
  0.6 21.8 %copy-start.2 = (f32[8,16,512]{2,1,0:T(8,128)S(1)}, f32[8,16,512]{2,1,0:T(8,128)}, u32[]{:S(2)}) copy-start(f32[8,16,512]{2,1,0:T(8,128)} %param.6) | copy-start | bytes 786436
  0.6 21.8 %copy-start.3 = (f32[8,16,512]{2,1,0:T(8,128)S(1)}, f32[8,16,512]{2,1,0:T(8,128)}, u32[]{:S(2)}) copy-start(f32[8,16,512]{2,1,0:T(8,128)} %param.5) | copy-start | bytes 786436
  1.7 7.2 %collective-permute-start = (f32[2,2,16,512]{3,2,1,0:T(8,128)S(1)}, f32[2,2,16,512]{3,2,1,0:T(8,128)S(1)}, u32[]{:S(2)}, u32[]{:S(2)}) collective-permute-start(f32[2,2,16,512]{3,2,1,0:T(8,128)S(1)} %get-tuple-element.80), channel_id=1, source_target_pairs={{0,2},{2,4},{4,6},{6,8},{8,10},{10,12},{12,14},{14,16},{16,18},{18... | collective-permute-start | bytes 393224 | tf_op jit(solution)/shard_map/ppermute | solution.py:30
  3.6 7.0 %collective-permute-start.1 = (f32[2,2,16,512]{3,2,1,0:T(8,128)S(1)}, f32[2,2,16,512]{3,2,1,0:T(8,128)S(1)}, u32[]{:S(2)}, u32[]{:S(2)}) collective-permute-start(f32[2,2,16,512]{3,2,1,0:T(8,128)S(1)} %get-tuple-element.81), channel_id=1, source_target_pairs={{2,0},{4,2},{6,4},{8,6},{10,8},{12,10},{14,12},{16,14},{18,16},{20... | collective-permute-start | bytes 393224 | tf_op jit(solution)/shard_map/ppermute | solution.py:32
  11.8 6.5 %collective-permute-start.2 = (f32[2,12,2,512]{3,2,1,0:T(2,128)S(1)}, f32[2,12,2,512]{3,2,1,0:T(2,128)S(1)}, u32[]{:S(2)}, u32[]{:S(2)}) collective-permute-start(f32[2,12,2,512]{3,2,1,0:T(2,128)S(1)} %get-tuple-element.70), channel_id=1, source_target_pairs={{0,1},{2,3},{4,5},{6,7},{8,9},{10,11},{12,13},{14,15},{16,17},{18,... | collective-permute-start | bytes 294920 | tf_op jit(solution)/shard_map/ppermute | solution.py:30
  15.3 7.1 %collective-permute-start.3 = (f32[2,12,2,512]{3,2,1,0:T(2,128)S(1)}, f32[2,12,2,512]{3,2,1,0:T(2,128)S(1)}, u32[]{:S(2)}, u32[]{:S(2)}) collective-permute-start(f32[2,12,2,512]{3,2,1,0:T(2,128)S(1)} %get-tuple-element.71), channel_id=1, source_target_pairs={{1,0},{3,2},{5,4},{7,6},{9,8},{11,10},{13,12},{15,14},{17,16},{19,... | collective-permute-start | bytes 294920 | tf_op jit(solution)/shard_map/ppermute | solution.py:32
  23.8 1.0 copy-start
  25.8 12.0 %copy-start.1 = (f32[8,16,512]{2,1,0:T(8,128)S(1)}, f32[8,16,512]{2,1,0:T(8,128)}, u32[]{:S(2)}) copy-start(f32[8,16,512]{2,1,0:T(8,128)} %param.9) | copy-start | bytes 786436
  25.8 7.3 %collective-permute-start.4 = (f32[2,2,16,512]{3,2,1,0:T(8,128)S(1)}, f32[2,2,16,512]{3,2,1,0:T(8,128)S(1)}, u32[]{:S(2)}, u32[]{:S(2)}) collective-permute-start(f32[2,2,16,512]{3,2,1,0:T(8,128)S(1)} %get-tuple-element.78), channel_id=1, source_target_pairs={{0,2},{2,4},{4,6},{6,8},{8,10},{10,12},{12,14},{14,16},{16,18},{18... | collective-permute-start | bytes 393224 | tf_op jit(solution)/shard_map/ppermute | solution.py:30
  27.9 7.0 %collective-permute-start.5 = (f32[2,2,16,512]{3,2,1,0:T(8,128)S(1)}, f32[2,2,16,512]{3,2,1,0:T(8,128)S(1)}, u32[]{:S(2)}, u32[]{:S(2)}) collective-permute-start(f32[2,2,16,512]{3,2,1,0:T(8,128)S(1)} %get-tuple-element.79), channel_id=1, source_target_pairs={{2,0},{4,2},{6,4},{8,6},{10,8},{12,10},{14,12},{16,14},{18,16},{20... | collective-permute-start | bytes 393224 | tf_op jit(solution)/shard_map/ppermute | solution.py:32
  35.0 3.7 %collective-permute-start.6 = (f32[2,12,2,512]{3,2,1,0:T(2,128)S(1)}, f32[2,12,2,512]{3,2,1,0:T(2,128)S(1)}, u32[]{:S(2)}, u32[]{:S(2)}) collective-permute-start(f32[2,12,2,512]{3,2,1,0:T(2,128)S(1)} %get-tuple-element.68), channel_id=1, source_target_pairs={{0,1},{2,3},{4,5},{6,7},{8,9},{10,11},{12,13},{14,15},{16,17},{18,... | collective-permute-start | bytes 294920 | tf_op jit(solution)/shard_map/ppermute | solution.py:30
  36.5 6.5 %collective-permute-start.7 = (f32[2,12,2,512]{3,2,1,0:T(2,128)S(1)}, f32[2,12,2,512]{3,2,1,0:T(2,128)S(1)}, u32[]{:S(2)}, u32[]{:S(2)}) collective-permute-start(f32[2,12,2,512]{3,2,1,0:T(2,128)S(1)} %get-tuple-element.69), channel_id=1, source_target_pairs={{1,0},{3,2},{5,4},{7,6},{9,8},{11,10},{13,12},{15,14},{17,16},{19,... | collective-permute-start | bytes 294920 | tf_op jit(solution)/shard_map/ppermute | solution.py:32
  43.3 1.1 %copy-start.4 = (f32[8,16,512]{2,1,0:T(8,128)S(1)}, f32[8,16,512]{2,1,0:T(8,128)}, u32[]{:S(2)}) copy-start(f32[8,16,512]{2,1,0:T(8,128)} %param.8) | copy-start | bytes 786436
  50.2 7.9 %collective-permute-start.8 = (f32[2,2,20,512]{3,2,1,0:T(8,128)S(1)}, f32[2,2,20,512]{3,2,1,0:T(8,128)S(1)}, u32[]{:S(2)}, u32[]{:S(2)}) collective-permute-start(f32[2,2,20,512]{3,2,1,0:T(8,128)S(1)} %pad_maximum_fusion.9), channel_id=1, source_target_pairs={{0,2},{2,4},{4,6},{6,8},{8,10},{10,12},{12,14},{14,16},{16,18},{18... | collective-permute-start | bytes 491528 | tf_op jit(solution)/shard_map/ppermute | solution.py:19
  58.2 5.1 %collective-permute-start.9 = (f32[2,2,20,512]{3,2,1,0:T(8,128)S(1)}, f32[2,2,20,512]{3,2,1,0:T(8,128)S(1)}, u32[]{:S(2)}, u32[]{:S(2)}) collective-permute-start(f32[2,2,20,512]{3,2,1,0:T(8,128)S(1)} %get-tuple-element.57), channel_id=1, source_target_pairs={{2,0},{4,2},{6,4},{8,6},{10,8},{12,10},{14,12},{16,14},{18,16},{20... | collective-permute-start | bytes 491528 | tf_op jit(solution)/shard_map/ppermute | solution.py:19
  63.3 3.4 %collective-permute-start.10 = (f32[2,8,2,512]{3,2,1,0:T(2,128)S(1)}, f32[2,8,2,512]{3,2,1,0:T(2,128)S(1)}, u32[]{:S(2)}, u32[]{:S(2)}) collective-permute-start(f32[2,8,2,512]{3,2,1,0:T(2,128)S(1)} %pad_maximum_fusion.25), channel_id=1, source_target_pairs={{0,1},{2,3},{4,5},{6,7},{8,9},{10,11},{12,13},{14,15},{16,17},{18,... | collective-permute-start | bytes 196616 | tf_op jit(solution)/shard_map/ppermute | solution.py:19
  66.8 6.2 %collective-permute-start.11 = (f32[2,8,2,512]{3,2,1,0:T(2,128)S(1)}, f32[2,8,2,512]{3,2,1,0:T(2,128)S(1)}, u32[]{:S(2)}, u32[]{:S(2)}) collective-permute-start(f32[2,8,2,512]{3,2,1,0:T(2,128)S(1)} %get-tuple-element.65), channel_id=1, source_target_pairs={{1,0},{3,2},{5,4},{7,6},{9,8},{11,10},{13,12},{15,14},{17,16},{19,... | collective-permute-start | bytes 196616 | tf_op jit(solution)/shard_map/ppermute | solution.py:19
  79.8 7.9 %collective-permute-start.12 = (f32[2,2,20,512]{3,2,1,0:T(8,128)S(1)}, f32[2,2,20,512]{3,2,1,0:T(8,128)S(1)}, u32[]{:S(2)}, u32[]{:S(2)}) collective-permute-start(f32[2,2,20,512]{3,2,1,0:T(8,128)S(1)} %pad_maximum_fusion.7), channel_id=1, source_target_pairs={{0,2},{2,4},{4,6},{6,8},{8,10},{10,12},{12,14},{14,16},{16,18},{18... | collective-permute-start | bytes 491528 | tf_op jit(solution)/shard_map/ppermute | solution.py:19
  87.7 5.1 %collective-permute-start.13 = (f32[2,2,20,512]{3,2,1,0:T(8,128)S(1)}, f32[2,2,20,512]{3,2,1,0:T(8,128)S(1)}, u32[]{:S(2)}, u32[]{:S(2)}) collective-permute-start(f32[2,2,20,512]{3,2,1,0:T(8,128)S(1)} %get-tuple-element.55), channel_id=1, source_target_pairs={{2,0},{4,2},{6,4},{8,6},{10,8},{12,10},{14,12},{16,14},{18,16},{20... | collective-permute-start | bytes 491528 | tf_op jit(solution)/shard_map/ppermute | solution.py:19
  92.9 3.5 %collective-permute-start.14 = (f32[2,8,2,512]{3,2,1,0:T(2,128)S(1)}, f32[2,8,2,512]{3,2,1,0:T(2,128)S(1)}, u32[]{:S(2)}, u32[]{:S(2)}) collective-permute-start(f32[2,8,2,512]{3,2,1,0:T(2,128)S(1)} %pad_maximum_fusion.23), channel_id=1, source_target_pairs={{0,1},{2,3},{4,5},{6,7},{8,9},{10,11},{12,13},{14,15},{16,17},{18,... | collective-permute-start | bytes 196616 | tf_op jit(solution)/shard_map/ppermute | solution.py:19
  96.4 6.2 %collective-permute-start.15 = (f32[2,8,2,512]{3,2,1,0:T(2,128)S(1)}, f32[2,8,2,512]{3,2,1,0:T(2,128)S(1)}, u32[]{:S(2)}, u32[]{:S(2)}) collective-permute-start(f32[2,8,2,512]{3,2,1,0:T(2,128)S(1)} %get-tuple-element.63), channel_id=1, source_target_pairs={{1,0},{3,2},{5,4},{7,6},{9,8},{11,10},{13,12},{15,14},{17,16},{19,... | collective-permute-start | bytes 196616 | tf_op jit(solution)/shard_map/ppermute | solution.py:19
where the time goes:
time: 104 us
  waiting for transfers between devices  47.2 us (45%)
  starting transfers between devices  34.1 us (33%)
  other arithmetic  19.7 us (19%)
  local copies, waits for them, and re-layouts  1.55 us (1%)
  between operations  1.04 us (1%)
    ppermute x8, waiting for transfers between devices, from_behind(): return lax.ppermute(block, axis, route)  31.2 us
    ppermute x8, starting transfers between devices, from_behind(): return lax.ppermute(block, axis, route)  13.6 us
    ppermute x4, waiting for transfers between devices, extended(): lax.ppermute(head, axis, [((i + 1) % count, i) for i in range(ends)])  12 us
    ppermute x4, starting transfers between devices, extended(): lax.ppermute(head, axis, [((i + 1) % count, i) for i in range(ends)])  11.7 us
    ppermute x4, starting transfers between devices, extended(): lax.ppermute(tail, axis, [(i, (i + 1) % count) for i in range(ends)])  8.86 us
    neg x2, other arithmetic, advance_solver_step(): grad_x = 0.5 * (padded[1:-1, 1:-1, 2:] - padded[1:-1, 1:-1, :-2])  4.6 us
    ppermute x4, waiting for transfers between devices, extended(): lax.ppermute(tail, axis, [(i, (i + 1) % count) for i in range(ends)])  4 us
    neg x2, other arithmetic, advance_solver_step(): grad_y = 0.5 * (padded[1:-1, 2:, 1:-1] - padded[1:-1, :-2, 1:-1])  2.85 us
  transfers between devices with their start and end apart: 16, of which 16 were waited for; matrix products, arithmetic and copies ran while one was open for 0% of the time, Pallas kernels for 0%

commit v1 on v0

v1 whole, which is shorter than its diff:
```python
import functools
import math

import jax
import jax.numpy as jnp
from jax import lax
from jax.experimental import pallas as pl
from jax.experimental.pallas import tpu as pltpu
from jax.sharding import PartitionSpec as P

TIME_STEP = 0.15
ANISOTROPY = 0.05
GRAD_FLOOR = 0.01
LATENT_HEAT = 1.8
DRIVE_SCALE = 0.9
DRIVE_SHARP = 10.0
MELT_POINT = 1.0

BASE = 1.0 - 3.0 * ANISOTROPY
RISE = 4.0 * ANISOTROPY
HALF_BASE = 0.5 * BASE
FALL = 8.0 * ANISOTROPY - 0.5 * RISE
TWIST = 8.0 * ANISOTROPY
SLOPE_0 = RISE * HALF_BASE - FALL * BASE
SLOPE_1 = -2.0 * RISE * FALL
FLOOR = 4.0 * GRAD_FLOOR

ATAN = (
    1.0, -0.3333328366279602, 0.19998230040073395, -0.14261573553085327,
    0.10940198600292206, -0.08372063934803009, 0.05746355652809143,
    -0.030717508867383003, 0.010680719278752804, -0.0017437011701986194,
)

SIDES = ((1, 0), (-1, 0), (0, 1), (0, -1), (1, 1), (1, -1), (-1, 1), (-1, -1))
ROW = 8


def recip(x):
    r = pl.reciprocal(x, approx=True)
    return r * (2.0 - x * r)


def arctan(x):
    size = jnp.abs(x)
    big = size > 1.0
    y = jnp.where(big, recip(jnp.maximum(size, 1.0)), size)
    z = y * y
    total = jnp.full_like(z, ATAN[-1])
    for c in ATAN[-2::-1]:
        total = total * z + c
    total = total * y
    total = jnp.where(big, 0.5 * math.pi - total, total)
    return jnp.where(x < 0.0, -total, total)


def basis(dz, dy, dx):
    zz, yy, xx = dz * dz, dy * dy, dx * dx
    s = zz + yy + xx + FLOOR
    r = recip(s)
    qs = (zz * zz + yy * yy + xx * xx) * r
    q = qs * r
    a = BASE + RISE * q
    big_a = a * (HALF_BASE - FALL * q)
    big_b = TWIST * a * r
    return zz, yy, xx, r, qs, q, a, big_a, big_b


def flux_of(d, sq, b):
    return d * (b[7] + b[8] * sq)


def tangent(dz, dy, dx, ez, ey, ex, b):
    zz, yy, xx, r, qs, q, a, big_a, big_b = b
    mz, my, mx = dz * ez, dy * ey, dx * ex
    g = mz + my + mx
    t = zz * mz + yy * my + xx * mx
    dq = (4.0 * r * r) * (t - qs * g)
    d_a = (SLOPE_0 + SLOPE_1 * q) * dq
    d_b = r * (TWIST * RISE * dq - (2.0 * TWIST) * a * r * g)
    return big_a, 3.0 * big_b, d_a, d_b


def turn(d, sq, e, t):
    return (t[0] + t[1] * sq) * e + d * (t[2] + t[3] * sq)


def kernel(
    nz, ny,
    p_in, u_in, k_in, ps_in, ts_in,
    sp_out, st_out, gm_out,
    p0, p1, d1, d0, u0, t1, t0, u1,
    jz, jy, jx, gz, gy, gx,
    r0, rp0, ru0, r1, rp1, ru1, tl1, gr0, pb0,
    sy0, ry0, sy1, ry1, sy2, ry2, sy3, ry3,
    sc0, rc0, sc1, rc1, sc2, rc2,
    ssem, rsem,
):
    Z, Y, X = p_in.shape
    tiles = range(Y // 8)
    zi, yi = lax.axis_index("gz"), lax.axis_index("gy")

    def there(side):
        cond = None
        for step, at, count in ((side[0], zi, nz), (side[1], yi, ny)):
            if step:
                c = at < count - 1 if step > 0 else at > 0
                cond = c if cond is None else jnp.logical_and(cond, c)
        return cond

    def opposite(side):
        return (-side[0], -side[1])

    barrier = pltpu.get_barrier_semaphore()
    for side in SIDES:
        @pl.when(there(side))
        def _(side=side):
            pl.semaphore_signal(
                barrier, inc=1, device_id=(zi + side[0], yi + side[1]),
                device_id_type=pl.DeviceIdType.MESH,
            )

    slots = iter(range(1000))

    def message(side, src, dst):
        slot = next(slots)
        copy = pltpu.make_async_remote_copy(
            src_ref=src, dst_ref=dst, send_sem=ssem.at[slot], recv_sem=rsem.at[slot],
            device_id=(zi + side[0], yi + side[1]), device_id_type=pl.DeviceIdType.MESH,
        )
        return side, copy

    def start(messages):
        for side, copy in messages:
            pl.when(there(side))(copy.start)

    def arrive(messages):
        for side, copy in messages:
            pl.when(there(opposite(side)))(copy.wait_recv)

    def sent(messages):
        for side, copy in messages:
            pl.when(there(side))(copy.wait_send)

    own = pl.ds(ROW, Y)

    def thick(buf):
        return [
            message((1, 0), buf.at[pl.ds(Z, 2), own], buf.at[pl.ds(0, 2), own]),
            message((-1, 0), buf.at[pl.ds(2, 2), own], buf.at[pl.ds(Z + 2, 2), own]),
        ]

    def thin(buf):
        return [
            message((1, 0), buf.at[pl.ds(Z, 1), own], buf.at[pl.ds(0, 1), own]),
            message((-1, 0), buf.at[pl.ds(1, 1), own], buf.at[pl.ds(Z + 1, 1), own]),
        ]

    def along_y(src, dst):
        return [
            message((0, 1), src.at[1], dst.at[0]),
            message((0, -1), src.at[0], dst.at[1]),
        ]

    def corners(src, dst):
        return [message(side, src.at[i], dst.at[i]) for i, side in enumerate(SIDES[4:])]

    row = lax.broadcasted_iota(jnp.int32, (8, X), 0)
    col = lax.broadcasted_iota(jnp.int32, (8, X), 1)
    first, last = col == 0, col == X - 1
    lane = lax.broadcasted_iota(jnp.int32, (8, 128), 1)

    def left(x, fill=0.0):
        return jnp.where(first, fill, pltpu.roll(x, 1, 1))

    def right(x, fill=0.0):
        return jnp.where(last, fill, pltpu.roll(x, X - 1, 1))

    def rows(t, shift=0):
        return pl.ds(ROW + 8 * t + shift, 8)

    def pack(src, base, deep, dst, at):
        for z in range(Z):
            for k in range(deep):
                dst[0, at + k, pl.ds(z, 1), :] = src[base + z, pl.ds(ROW + k, 1), :]
                dst[1, at + k, pl.ds(z, 1), :] = src[base + z, pl.ds(ROW + Y - 1 - k, 1), :]

    def unpack(src, at, dst, base):
        for z in range(Z):
            dst[base + z, pl.ds(ROW - 1, 1), :] = src[0, at, pl.ds(z, 1), :]
            dst[base + z, pl.ds(ROW + Y, 1), :] = src[1, at, pl.ds(z, 1), :]

    def pack_corner(src, dst, at):
        for i, (sz, sy) in enumerate(SIDES[4:]):
            zc = Z + 1 if sz > 0 else 2
            yc = ROW + Y - 1 if sy > 0 else ROW
            dst[i, at] = src[zc, pl.ds(yc, 1), :]

    def unpack_corner(src, at, dst):
        for i, (sz, sy) in enumerate(SIDES[4:]):
            zc = 1 if sz > 0 else Z + 2
            yc = ROW - 1 if sy > 0 else ROW + Y
            dst[zc, pl.ds(yc, 1), :] = src[i, at]

    def diffs(buf, zc, t):
        c = buf[zc, rows(t), :]
        dz = buf[zc + 1, rows(t), :] - buf[zc - 1, rows(t), :]
        dy = buf[zc, rows(t, 1), :] - buf[zc, rows(t, -1), :]
        dx = right(c) - left(c)
        return c, dz, dy, dx

    def ring_diffs(buf, at, edge, edge_at, corner, corner_at, s):
        near, far, mine = buf[s, at], buf[s, at + 1], edge[s, edge_at]
        sy = 1 if s == 0 else -1
        lo = corner[SIDES[4:].index((1, sy)), corner_at]
        hi = corner[SIDES[4:].index((-1, sy)), corner_at]
        up = jnp.where(row == Z - 1, hi, pltpu.roll(near, Z - 1, 0))
        dn = jnp.where(row == 0, lo, pltpu.roll(near, 1, 0))
        dy = mine - far if s == 0 else far - mine
        return up - dn, dy, right(near) - left(near)

    def ends(c):
        return jnp.where(
            lane == 0, c[:, :128], jnp.where(lane == 127, c[:, X - 128:], 0.0)
        )

    def spread(e):
        return jnp.concatenate([e] * (X // 128), axis=1)

    def diff_flux(f, end):
        end = spread(end)
        return right(f, -end) - left(f, end)

    def end_basis(c):
        d = ends(c)
        xx = d * d
        r = recip(xx + FLOOR)
        qs = xx * xx * r
        q = qs * r
        a = BASE + RISE * q
        return d, xx, r, qs, q, a, a * (HALF_BASE - FALL * q), TWIST * a * r

    def end_flux(b):
        d, xx, r, qs, q, a, big_a, big_b = b
        return d * (big_a + big_b * xx)

    def end_tangent(b, e):
        d, xx, r, qs, q, a, big_a, big_b = b
        m = d * e
        dq = (4.0 * r * r) * (xx * m - qs * m)
        d_a = (SLOPE_0 + SLOPE_1 * q) * dq
        d_b = r * (TWIST * RISE * dq - (2.0 * TWIST) * a * r * m)
        return (big_a + 3.0 * big_b * xx) * e + d * (d_a + d_b * xx)

    def divergence(fz, fy, fx, z, t):
        total = fz[z + 2, pl.ds(8 * t, 8), :] - fz[z, pl.ds(8 * t, 8), :]
        total += fy[z, rows(t, 1), :] - fy[z, rows(t, -1), :]
        return 0.25 * (total + fx[z, pl.ds(8 * t, 8), :])

    def laplacian(buf, zc, t):
        c = buf[zc, rows(t), :]
        total = buf[zc + 1, rows(t), :] + buf[zc - 1, rows(t), :]
        total += buf[zc, rows(t, 1), :] + buf[zc, rows(t, -1), :]
        return c, total + right(c) + left(c) - 6.0 * c

    def reaction(p, u):
        x = DRIVE_SHARP * (MELT_POINT - u)
        m = DRIVE_SCALE / math.pi * arctan(x)
        well = p * (1.0 - p)
        tilt = p - 0.5 + m
        slope = (-DRIVE_SHARP * DRIVE_SCALE / math.pi) * recip(1.0 + x * x)
        return well * tilt, (1.0 - 2.0 * p) * tilt + well, well * slope

    def over_z(body):
        def step(z, carry):
            for t in tiles:
                body(z, t)
            return carry
        lax.fori_loop(0, Z, step, 0)

    def cells(t):
        return pl.ds(8 * t, 8)

    m_p0 = thick(p0)
    m_y0 = along_y(sy0, ry0)
    m_c0 = corners(sc0, rc0)
    m_u0 = thin(u0)
    m_d1 = thick(d1)
    m_t1 = thin(t1)
    m_y1 = along_y(sy1, ry1)
    m_p1 = thick(p1)
    m_y2 = along_y(sy2, ry2)
    m_c1 = corners(sc1, rc1)
    m_d0 = thick(d0)
    m_t0 = thin(t0)
    m_y3 = along_y(sy3, ry3)
    m_c2 = corners(sc2, rc2)

    def load(z, t):
        p0[z + 2, rows(t), :] = p_in[z, cells(t), :]
        u0[z + 1, rows(t), :] = u_in[z, cells(t), :]
        ts = ts_in[z, cells(t), :]
        t1[z + 1, rows(t), :] = ts
        w = ps_in[z, cells(t), :] + LATENT_HEAT * ts
        d1[z + 2, rows(t), :] = TIME_STEP * k_in[z, cells(t), :] * w
    over_z(load)
    pack(p0, 2, 2, sy0, 0)
    pack(u0, 1, 1, sy0, 2)
    pack_corner(p0, sc0, 0)
    pack_corner(d1, sc0, 1)
    pack(d1, 2, 2, sy1, 0)
    pack(t1, 1, 1, sy1, 2)

    @pl.when(zi == 0)
    def _():
        for buf in (p0, p1, d1, d0):
            buf[pl.ds(0, 2)] = jnp.zeros((2,) + buf.shape[1:], jnp.float32)
        for buf in (u0, t1, t0):
            buf[0] = jnp.zeros(buf.shape[1:], jnp.float32)

    @pl.when(zi == nz - 1)
    def _():
        for buf in (p0, p1, d1, d0):
            buf[pl.ds(Z + 2, 2)] = jnp.zeros((2,) + buf.shape[1:], jnp.float32)
        for buf in (u0, t1, t0):
            buf[Z + 1] = jnp.zeros(buf.shape[1:], jnp.float32)

    for s, at_end in ((0, yi == 0), (1, yi == ny - 1)):
        @pl.when(at_end)
        def _(s=s):
            for buf in (ry0, ry1, ry2, ry3):
                buf[s] = jnp.zeros(buf.shape[1:], jnp.float32)

    for i, side in enumerate(SIDES[4:]):
        @pl.when(jnp.logical_not(there(opposite(side))))
        def _(i=i):
            for buf in (rc0, rc1, rc2):
                buf[i] = jnp.zeros(buf.shape[1:], jnp.float32)

    def one(cond):
        return jnp.where(cond, 1, 0)

    near_z = one(zi > 0) + one(zi < nz - 1)
    near_y = one(yi > 0) + one(yi < ny - 1)
    pl.semaphore_wait(barrier, near_z + near_y + near_z * near_y)
    start(m_y0 + m_p0 + m_c0 + m_u0 + m_y1 + m_d1 + m_t1)

    def first_terms(z, t):
        p, u = p_in[z, cells(t), :], u_in[z, cells(t), :]
        r0[z, cells(t), :], rp0[z, cells(t), :], ru0[z, cells(t), :] = reaction(p, u)
    over_z(first_terms)

    arrive(m_y0 + m_c0)
    unpack(ry0, 0, p0, 2)
    unpack(ry0, 2, u0, 1)
    unpack_corner(rc0, 0, p0)
    arrive(m_p0 + m_u0)

    def put_ring(f, s, dst):
        at = ROW - 1 if s == 0 else ROW + Y
        for z in range(Z):
            dst[z, pl.ds(at, 1), :] = f[z:z + 1, :]

    def forward_flux(buf, zc, t):
        c, dz, dy, dx = diffs(buf, zc, t)
        b = basis(dz, dy, dx)
        return c, (dz, dy, dx), b

    def flux0(z, t):
        c, (dz, dy, dx), b = forward_flux(p0, z + 2, t)
        jz[z + 1, cells(t), :] = flux_of(dz, b[0], b)
        jy[z, rows(t), :] = flux_of(dy, b[1], b)
        jx[z, cells(t), :] = diff_flux(flux_of(dx, b[2], b), end_flux(end_basis(c)))
    over_z(flux0)
    for zc in (1, Z + 2):
        for t in tiles:
            _, (dz, dy, dx), b = forward_flux(p0, zc, t)
            jz[zc - 1, cells(t), :] = flux_of(dz, b[0], b)
    for s in (0, 1):
        dz, dy, dx = ring_diffs(ry0, 0, sy0, 0, rc0, 0, s)
        b = basis(dz, dy, dx)
        put_ring(flux_of(dy, b[1], b), s, jy)

    def advance(z, t):
        growth = divergence(jz, jy, jx, z, t) + r0[z, cells(t), :]
        gr0[z, cells(t), :] = growth
        p = p_in[z, cells(t), :]
        gain = TIME_STEP * k_in[z, cells(t), :] * growth
        p1[z + 2, rows(t), :] = p + gain
        u, lap = laplacian(u0, z + 1, t)
        u1[z, cells(t), :] = u + TIME_STEP * lap + LATENT_HEAT * gain
    over_z(advance)
    pack(p1, 2, 2, sy2, 0)
    pack_corner(p1, sc1, 0)
    start(m_y2 + m_p1 + m_c1)

    arrive(m_y1 + m_d1 + m_t1)
    unpack(ry1, 0, d1, 2)
    unpack(ry1, 2, t1, 1)
    unpack_corner(rc0, 1, d1)

    def second_terms(z, t):
        p, u = p1[z + 2, rows(t), :], u1[z, cells(t), :]
        r1[z, cells(t), :], rp1[z, cells(t), :], ru1[z, cells(t), :] = reaction(p, u)
        ts, lap = laplacian(t1, z + 1, t)
        tl1[z, cells(t), :] = ts + TIME_STEP * lap
    over_z(second_terms)

    arrive(m_y2 + m_c1)
    unpack(ry2, 0, p1, 2)
    unpack_corner(rc1, 0, p1)
    arrive(m_p1)

    def adjoint_flux(p, d, with_flux):
        def body(z, t):
            c, (dz, dy, dx), b = forward_flux(p, z + 2, t)
            e, ez, ey, ex = diffs(d, z + 2, t)
            k = tangent(dz, dy, dx, ez, ey, ex, b)
            eb = end_basis(c)
            gz[z + 1, cells(t), :] = turn(dz, b[0], ez, k)
            gy[z, rows(t), :] = turn(dy, b[1], ey, k)
            gx[z, cells(t), :] = diff_flux(turn(dx, b[2], ex, k), end_tangent(eb, ends(e)))
            if with_flux:
                jz[z + 1, cells(t), :] = flux_of(dz, b[0], b)
                jy[z, rows(t), :] = flux_of(dy, b[1], b)
                jx[z, cells(t), :] = diff_flux(flux_of(dx, b[2], b), end_flux(eb))
        over_z(body)
        for zc in (1, Z + 2):
            for t in tiles:
                _, (dz, dy, dx), b = forward_flux(p, zc, t)
                _, ez, ey, ex = diffs(d, zc, t)
                k = tangent(dz, dy, dx, ez, ey, ex, b)
                gz[zc - 1, cells(t), :] = turn(dz, b[0], ez, k)
                if with_flux:
                    jz[zc - 1, cells(t), :] = flux_of(dz, b[0], b)

    def adjoint_ring(p_args, d_args, with_flux):
        for s in (0, 1):
            dz, dy, dx = ring_diffs(*p_args, s)
            ez, ey, ex = ring_diffs(*d_args, s)
            b = basis(dz, dy, dx)
            k = tangent(dz, dy, dx, ez, ey, ex, b)
            put_ring(turn(dy, b[1], ey, k), s, gy)
            if with_flux:
                put_ring(flux_of(dy, b[1], b), s, jy)

    adjoint_flux(p1, d1, True)
    adjoint_ring((ry2, 0, sy2, 0, rc1, 0), (ry1, 0, sy1, 0, rc0, 1), True)

    def middle(z, t):
        d = d1[z + 2, rows(t), :]
        pb = ps_in[z, cells(t), :] + d * rp1[z, cells(t), :] + divergence(gz, gy, gx, z, t)
        ub = tl1[z, cells(t), :] + d * ru1[z, cells(t), :]
        pb0[z, cells(t), :] = pb
        t0[z + 1, rows(t), :] = ub
        d0[z + 2, rows(t), :] = TIME_STEP * k_in[z, cells(t), :] * (pb + LATENT_HEAT * ub)
    over_z(middle)
    pack(d0, 2, 2, sy3, 0)
    pack(t0, 1, 1, sy3, 2)
    pack_corner(d0, sc2, 0)
    start(m_y3 + m_d0 + m_c2 + m_t0)

    def mobility(z, t):
        growth = divergence(jz, jy, jx, z, t) + r1[z, cells(t), :]
        late = ps_in[z, cells(t), :] + LATENT_HEAT * ts_in[z, cells(t), :]
        early = pb0[z, cells(t), :] + LATENT_HEAT * t0[z + 1, rows(t), :]
        gm_out[z, cells(t), :] = TIME_STEP * (late * growth + early * gr0[z, cells(t), :])
    over_z(mobility)

    arrive(m_y3 + m_c2)
    unpack(ry3, 0, d0, 2)
    unpack(ry3, 2, t0, 1)
    unpack_corner(rc2, 0, d0)
    arrive(m_d0 + m_t0)
    adjoint_flux(p0, d0, False)
    adjoint_ring((ry0, 0, sy0, 0, rc0, 0), (ry3, 0, sy3, 0, rc2, 0), False)

    def finish(z, t):
        d = d0[z + 2, rows(t), :]
        sp_out[z, cells(t), :] = (
            pb0[z, cells(t), :] + d * rp0[z, cells(t), :] + divergence(gz, gy, gx, z, t)
        )
        ub, lap = laplacian(t0, z + 1, t)
        st_out[z, cells(t), :] = ub + TIME_STEP * lap + d * ru0[z, cells(t), :]
    over_z(finish)

    sent(
        m_p0 + m_y0 + m_c0 + m_u0 + m_d1 + m_t1 + m_y1
        + m_p1 + m_y2 + m_c1 + m_d0 + m_t0 + m_y3 + m_c2
    )


def body(nz, ny, *blocks):
    Z, Y, X = blocks[0].shape

    def buf(*shape):
        return pltpu.VMEM(shape, jnp.float32)

    wide = Y + 2 * ROW
    thick, thin, flat = (Z + 4, wide, X), (Z + 2, wide, X), (Z, Y, X)
    flux = [(Z + 2, Y, X), (Z, wide, X), (Z, Y, X)]
    scratch = [buf(*thick)] * 4 + [buf(*thin)] * 3 + [buf(*flat)]
    scratch += [buf(*s) for s in flux] * 2
    scratch += [buf(*flat)] * 9
    scratch += [buf(2, n, Z, X) for n in (3, 3, 3, 3, 2, 2, 3, 3)]
    scratch += [buf(4, n, 1, X) for n in (2, 2, 1, 1, 1, 1)]
    count = 36
    scratch += [pltpu.SemaphoreType.DMA((count,))] * 2
    vmem = pl.BlockSpec(memory_space=pltpu.VMEM)
    out = jax.ShapeDtypeStruct((Z, Y, X), jnp.float32)
    return pl.pallas_call(
        functools.partial(kernel, nz, ny),
        out_shape=(out, out, out),
        in_specs=[vmem] * 5,
        out_specs=(vmem, vmem, vmem),
        scratch_shapes=scratch,
        compiler_params=pltpu.CompilerParams(
            collective_id=0, has_side_effects=True, vmem_limit_bytes=40 * 1024 * 1024
        ),
    )(*blocks)


def solution(mesh):
    spec = P("gz", "gy", None)
    return jax.shard_map(
        functools.partial(body, mesh.shape["gz"], mesh.shape["gy"]),
        mesh=mesh,
        in_specs=(spec,) * 5,
        out_specs=(spec,) * 3,
        check_vma=False,
    )
```

time: 104 us -> 31.5 us (0.30)
  the two profiles are of different devices: /device:TPU:8 before, /device:TPU:9 now
where the time goes in v1:
time: 31.5 us; the launch traced here: 31.2 us
  Pallas kernels  23.7 us (75%)
  local copies, waits for them, and re-layouts  6.85 us (22%)
  between operations  0.65 us (2%)
    pallas_call x1, Pallas kernels, body(): pl.pallas_call(functools.partial(kernel, nz, ny), out_shape=(out, out, ou...  23.7 us
    unnamed x13, local copies, waits for them, and re-layouts  6.85 us

profile of v1, /device:TPU:9, one launch (start us, length us, event | category | flops | bytes accessed | tf_op | source)
XLA Modules:
  0.0 31.2 jit_solution(14780957496000232658)
XLA Ops:
  0.6 0.0 copy-start
  0.6 0.9 %copy-done = f32[8,16,512]{2,1,0:T(8,128)S(1)} copy-done((f32[8,16,512]{2,1,0:T(8,128)S(1)}, f32[8,16,512]{2,1,0:T(8,128)}, u32[]{:S(2)}) %copy-start) | copy-done | bytes 262168
  1.6 0.0 copy-start.1
  1.6 0.9 %copy-done.1 = f32[8,16,512]{2,1,0:T(8,128)S(1)} copy-done((f32[8,16,512]{2,1,0:T(8,128)S(1)}, f32[8,16,512]{2,1,0:T(8,128)}, u32[]{:S(2)}) %copy-start.1) | copy-done | bytes 262168
  2.5 0.0 copy-start.2
  2.5 0.9 %copy-done.2 = f32[8,16,512]{2,1,0:T(8,128)S(1)} copy-done((f32[8,16,512]{2,1,0:T(8,128)S(1)}, f32[8,16,512]{2,1,0:T(8,128)}, u32[]{:S(2)}) %copy-start.2) | copy-done | bytes 262168
  3.5 0.0 copy-start.3
  3.5 0.9 %copy-done.3 = f32[8,16,512]{2,1,0:T(8,128)S(1)} copy-done((f32[8,16,512]{2,1,0:T(8,128)S(1)}, f32[8,16,512]{2,1,0:T(8,128)}, u32[]{:S(2)}) %copy-start.3) | copy-done | bytes 262168
  4.4 0.0 copy-start.4
  4.4 0.9 %copy-done.4 = f32[8,16,512]{2,1,0:T(8,128)S(1)} copy-done((f32[8,16,512]{2,1,0:T(8,128)S(1)}, f32[8,16,512]{2,1,0:T(8,128)}, u32[]{:S(2)}) %copy-start.4) | copy-done | bytes 262168
  5.4 23.7 %shard_map.76 = (f32[8,16,512]{2,1,0:T(8,128)S(1)}, f32[8,16,512]{2,1,0:T(8,128)S(1)}, f32[8,16,512]{2,1,0:T(8,128)S(1)}) custom-call(f32[8,16,512]{2,1,0:T(8,128)S(1)} %copy-done, f32[8,16,512]{2,1,0:T(8,128)S(1)} %copy-done.1, f32[8,16,512]{2,1,0:T(8,128)S(1)} %copy-done.2, f32[8,16,512]{2,1,0:T(8,128)S(1)} %copy-done.3, f32[8,16,512]{2,1,0:T(8,128)S(1)} %copy-done.4), custom_call_target="tpu_custom_call" | custom-call | tf_op jit(solution)/shard_map/pallas_call | solution.py:510
  29.1 0.7 %copy.11 = f32[8,16,512]{2,1,0:T(8,128)} copy(f32[8,16,512]{2,1,0:T(8,128)S(1)} %get-tuple-element.6) | data formatting | bytes 524288
  29.8 0.7 %copy.12 = f32[8,16,512]{2,1,0:T(8,128)} copy(f32[8,16,512]{2,1,0:T(8,128)S(1)} %get-tuple-element.7) | data formatting | bytes 524288
  30.5 0.7 %copy.13 = f32[8,16,512]{2,1,0:T(8,128)} copy(f32[8,16,512]{2,1,0:T(8,128)S(1)} %get-tuple-element.8) | data formatting | bytes 524288
Async XLA Ops:
  0.6 1.0 %copy-start = (f32[8,16,512]{2,1,0:T(8,128)S(1)}, f32[8,16,512]{2,1,0:T(8,128)}, u32[]{:S(2)}) copy-start(f32[8,16,512]{2,1,0:T(8,128)} %p_in.1) | copy-start | bytes 786436
  1.6 0.9 %copy-start.1 = (f32[8,16,512]{2,1,0:T(8,128)S(1)}, f32[8,16,512]{2,1,0:T(8,128)}, u32[]{:S(2)}) copy-start(f32[8,16,512]{2,1,0:T(8,128)} %u_in.1) | copy-start | bytes 786436
  2.5 0.9 %copy-start.2 = (f32[8,16,512]{2,1,0:T(8,128)S(1)}, f32[8,16,512]{2,1,0:T(8,128)}, u32[]{:S(2)}) copy-start(f32[8,16,512]{2,1,0:T(8,128)} %k_in.1) | copy-start | bytes 786436
  3.5 0.9 %copy-start.3 = (f32[8,16,512]{2,1,0:T(8,128)S(1)}, f32[8,16,512]{2,1,0:T(8,128)}, u32[]{:S(2)}) copy-start(f32[8,16,512]{2,1,0:T(8,128)} %ps_in.1) | copy-start | bytes 786436
  4.4 0.9 %copy-start.4 = (f32[8,16,512]{2,1,0:T(8,128)S(1)}, f32[8,16,512]{2,1,0:T(8,128)}, u32[]{:S(2)}) copy-start(f32[8,16,512]{2,1,0:T(8,128)} %ts_in.1) | copy-start | bytes 786436

commit v2 on v1

v2 whole, which is shorter than its diff:
```python
import functools
import math

import jax
import jax.numpy as jnp
from jax import lax
from jax.experimental import pallas as pl
from jax.experimental.pallas import tpu as pltpu
from jax.sharding import PartitionSpec as P

TIME_STEP = 0.15
ANISOTROPY = 0.05
GRAD_FLOOR = 0.01
LATENT_HEAT = 1.8
DRIVE_SCALE = 0.9
DRIVE_SHARP = 10.0
MELT_POINT = 1.0

BASE = 1.0 - 3.0 * ANISOTROPY
RISE = 4.0 * ANISOTROPY
HALF_BASE = 0.5 * BASE
FALL = 8.0 * ANISOTROPY - 0.5 * RISE
TWIST = 8.0 * ANISOTROPY
SLOPE_0 = RISE * HALF_BASE - FALL * BASE
SLOPE_1 = -2.0 * RISE * FALL
FLOOR = 4.0 * GRAD_FLOOR

ATAN = (
    1.0, -0.3333328366279602, 0.19998230040073395, -0.14261573553085327,
    0.10940198600292206, -0.08372063934803009, 0.05746355652809143,
    -0.030717508867383003, 0.010680719278752804, -0.0017437011701986194,
)

SIDES = ((1, 0), (-1, 0), (0, 1), (0, -1), (1, 1), (1, -1), (-1, 1), (-1, -1))


def recip(x):
    r = pl.reciprocal(x, approx=True)
    return r * (2.0 - x * r)


def arctan(x):
    size = jnp.abs(x)
    big = size > 1.0
    y = jnp.where(big, recip(jnp.maximum(size, 1.0)), size)
    z = y * y
    total = jnp.full_like(z, ATAN[-1])
    for c in ATAN[-2::-1]:
        total = total * z + c
    total = total * y
    total = jnp.where(big, 0.5 * math.pi - total, total)
    return jnp.where(x < 0.0, -total, total)


def basis(dz, dy, dx):
    zz, yy, xx = dz * dz, dy * dy, dx * dx
    s = zz + yy + xx + FLOOR
    r = recip(s)
    qs = (zz * zz + yy * yy + xx * xx) * r
    q = qs * r
    a = BASE + RISE * q
    big_a = a * (HALF_BASE - FALL * q)
    big_b = TWIST * a * r
    return zz, yy, xx, r, qs, q, a, big_a, big_b


def flux_of(d, sq, b):
    return d * (b[7] + b[8] * sq)


def tangent(dz, dy, dx, ez, ey, ex, b):
    zz, yy, xx, r, qs, q, a, big_a, big_b = b
    mz, my, mx = dz * ez, dy * ey, dx * ex
    g = mz + my + mx
    t = zz * mz + yy * my + xx * mx
    dq = (4.0 * r * r) * (t - qs * g)
    d_a = (SLOPE_0 + SLOPE_1 * q) * dq
    d_b = r * (TWIST * RISE * dq - (2.0 * TWIST) * a * r * g)
    return big_a, 3.0 * big_b, d_a, d_b


def turn(d, sq, e, t):
    return (t[0] + t[1] * sq) * e + d * (t[2] + t[3] * sq)


def kernel(
    nz, ny,
    p_in, u_in, k_in, ps_in, ts_in,
    sp_out, st_out, gm_out,
    p0, p1, d1, d0, u0, t1, t0, u1, kb, sb,
    jz, jxy, gz, gxy,
    r0, rp0, ru0, r1, rp1, ru1, tl1, gr0, pb0,
    ring_j, ring_g,
    sy0, ry0, sy1, ry1, sy2, ry2, sy3, ry3,
    sc0, rc0, sc1, rc1, sc2, rc2, sc3, rc3,
    ssem, rsem, lsem,
):
    Z, Y, X = p_in.shape
    T, C = Y // 8, X // 128
    zi, yi = lax.axis_index("gz"), lax.axis_index("gy")

    def there(side):
        cond = None
        for step, at, count in ((side[0], zi, nz), (side[1], yi, ny)):
            if step:
                c = at < count - 1 if step > 0 else at > 0
                cond = c if cond is None else jnp.logical_and(cond, c)
        return cond

    def opposite(side):
        return (-side[0], -side[1])

    barrier = pltpu.get_barrier_semaphore()
    for side in SIDES:
        @pl.when(there(side))
        def _(side=side):
            pl.semaphore_signal(
                barrier, inc=1, device_id=(zi + side[0], yi + side[1]),
                device_id_type=pl.DeviceIdType.MESH,
            )

    local = [
        pltpu.make_async_copy(src, dst, lsem.at[i])
        for i, (src, dst) in enumerate((
            (p_in, p0.at[pl.ds(2, Z)]),
            (k_in, kb),
            (ps_in, sb),
            (ts_in, t1.at[pl.ds(1, Z)]),
            (u_in, u0.at[pl.ds(1, Z)]),
        ))
    ]
    for copy in local:
        copy.start()

    slots = iter(range(1000))

    def message(side, src, dst):
        slot = next(slots)
        copy = pltpu.make_async_remote_copy(
            src_ref=src, dst_ref=dst, send_sem=ssem.at[slot], recv_sem=rsem.at[slot],
            device_id=(zi + side[0], yi + side[1]), device_id_type=pl.DeviceIdType.MESH,
        )
        return side, copy

    def start(messages):
        for side, copy in messages:
            pl.when(there(side))(copy.start)

    def arrive(messages):
        for side, copy in messages:
            pl.when(there(opposite(side)))(copy.wait_recv)

    def sent(messages):
        for side, copy in messages:
            pl.when(there(side))(copy.wait_send)

    def thick(buf):
        return [
            message((1, 0), buf.at[pl.ds(Z, 2)], buf.at[pl.ds(0, 2)]),
            message((-1, 0), buf.at[pl.ds(2, 2)], buf.at[pl.ds(Z + 2, 2)]),
        ]

    def thin(buf):
        return [
            message((1, 0), buf.at[pl.ds(Z, 1)], buf.at[pl.ds(0, 1)]),
            message((-1, 0), buf.at[pl.ds(1, 1)], buf.at[pl.ds(Z + 1, 1)]),
        ]

    def along_y(src, dst):
        return [
            message((0, 1), src.at[1], dst.at[0]),
            message((0, -1), src.at[0], dst.at[1]),
        ]

    def corners(src, dst):
        return [message(side, src.at[i], dst.at[i]) for i, side in enumerate(SIDES[4:])]

    lane = lax.broadcasted_iota(jnp.int32, (8, 128), 1)
    row = lax.broadcasted_iota(jnp.int32, (8, 128), 0)
    top, bottom = row == 0, row == 7
    first, last = lane == 0, lane == 127

    def block(j):
        return pl.ds(128 * j, 128)

    def layer(buf, z):
        return [[buf[z, pl.ds(8 * t, 8), block(j)] for j in range(C)] for t in range(T)]

    def store(buf, z, t, j, value):
        buf[z, pl.ds(8 * t, 8), block(j)] = value

    def wide_row(buf, *at):
        return [
            jnp.broadcast_to(buf[(*at[:-1], pl.ds(at[-1], 1), block(j))], (8, 128))
            for j in range(C)
        ]

    def shift_x(row_of_tiles, end=None):
        before = [pltpu.roll(c, 1, 1) for c in row_of_tiles]
        after = [pltpu.roll(c, 127, 1) for c in row_of_tiles]
        zero = 0.0
        lo = [
            jnp.where(first, before[j - 1] if j else (zero if end is None else end), before[j])
            for j in range(C)
        ]
        hi = [
            jnp.where(
                last, after[j + 1] if j < C - 1 else (zero if end is None else -end), after[j]
            )
            for j in range(C)
        ]
        return lo, hi

    def shift_y(tiles, lo, hi):
        before = [[pltpu.roll(c, 1, 0) for c in r] for r in tiles]
        after = [[pltpu.roll(c, 7, 0) for c in r] for r in tiles]
        down = [
            [jnp.where(top, before[t - 1][j] if t else lo[j], before[t][j]) for j in range(C)]
            for t in range(T)
        ]
        up = [
            [jnp.where(bottom, after[t + 1][j] if t < T - 1 else hi[j], after[t][j]) for j in range(C)]
            for t in range(T)
        ]
        return down, up

    def sub(a, b):
        if isinstance(a, list):
            return [sub(x, y) for x, y in zip(a, b)]
        return a - b

    def diffs(buf, zc, lo, hi):
        c = layer(buf, zc)
        dz = sub(layer(buf, zc + 1), layer(buf, zc - 1))
        down, up = shift_y(c, lo, hi)
        sides = [shift_x(r) for r in c]
        return c, dz, sub(up, down), [sub(h, l) for l, h in sides]

    def halo_rows(rim, at, z):
        at = () if at is None else (at,)
        lo = [pltpu.roll(rim[(0, *at, slice(None), block(j))], lax.rem(Z - z, 8), 0) for j in range(C)]
        hi = [pltpu.roll(rim[(1, *at, slice(None), block(j))], 7 - z, 0) for j in range(C)]
        return lo, hi

    def corner_rows(corner, at, below):
        sz = 1 if below else -1
        lo = SIDES[4:].index((sz, 1))
        hi = SIDES[4:].index((sz, -1))
        return wide_row(corner, lo, at, 0), wide_row(corner, hi, at, 0)

    def ring_diffs(rim, at, edge, edge_at, corner, corner_at, s):
        near = [rim[s, at, :, block(j)] for j in range(C)]
        far = [rim[s, at + 1, :, block(j)] for j in range(C)]
        mine = [edge[s, edge_at, :, block(j)] for j in range(C)]
        sy = 1 if s == 0 else -1
        lo = wide_row(corner, SIDES[4:].index((1, sy)), corner_at, 0)
        hi = wide_row(corner, SIDES[4:].index((-1, sy)), corner_at, 0)
        (dn,), (up,) = ring_shift(near, lo, hi)
        l, h = shift_x(near)
        dy = sub(mine, far) if s == 0 else sub(far, mine)
        return sub(up, dn), dy, sub(h, l)

    def ring_shift(near, lo, hi):
        down = [jnp.where(top, lo[j], pltpu.roll(near[j], 1, 0)) for j in range(C)]
        up = [jnp.where(bottom, hi[j], pltpu.roll(near[j], 7, 0)) for j in range(C)]
        return [down], [up]

    def pack(src, base, deep, dst, at):
        for k in range(deep):
            for s, y in ((0, k), (1, Y - 1 - k)):
                total = wide_row(src, base, y)
                for z in range(1, Z):
                    now = wide_row(src, base + z, y)
                    total = [jnp.where(row == z, n, o) for n, o in zip(now, total)]
                for j in range(C):
                    dst[s, at + k, :, block(j)] = total[j]

    def pack_corner(src, dst):
        for i, (sz, sy) in enumerate(SIDES[4:]):
            zc = Z + 1 if sz > 0 else 2
            yc = Y - 1 if sy > 0 else 0
            dst[i, 0] = src[zc, pl.ds(yc, 1), :]

    def ends(tiles):
        return jnp.where(first, tiles[0], jnp.where(last, tiles[C - 1], 0.0))

    def end_basis(d):
        xx = d * d
        r = recip(xx + FLOOR)
        qs = xx * xx * r
        q = qs * r
        a = BASE + RISE * q
        return d, xx, r, qs, q, a, a * (HALF_BASE - FALL * q), TWIST * a * r

    def end_flux(b):
        d, xx, r, qs, q, a, big_a, big_b = b
        return d * (big_a + big_b * xx)

    def end_tangent(b, e):
        d, xx, r, qs, q, a, big_a, big_b = b
        m = d * e
        dq = (4.0 * r * r) * (xx * m - qs * m)
        d_a = (SLOPE_0 + SLOPE_1 * q) * dq
        d_b = r * (TWIST * RISE * dq - (2.0 * TWIST) * a * r * m)
        return (big_a + 3.0 * big_b * xx) * e + d * (d_a + d_b * xx)

    def cross(fx, fy, end, lo, hi):
        out = []
        down, up = shift_y(fy, lo, hi)
        for t in range(T):
            l, h = shift_x(fx[t], end[t])
            out.append([(h[j] - l[j]) + (up[t][j] - down[t][j]) for j in range(C)])
        return out

    def blank():
        return [[None] * C for _ in range(T)]

    def flux_layer(p, zc, p_rows, d=None, d_rows=None, with_flux=True, ring=None):
        c, dz, dy, dx = diffs(p, zc, *p_rows)
        if d is not None:
            e, ez, ey, ex = diffs(d, zc, *d_rows)
        fx, fy, hx, hy = blank(), blank(), blank(), blank()
        for t in range(T):
            for j in range(C):
                a = (dz[t][j], dy[t][j], dx[t][j])
                b = basis(*a)
                if with_flux:
                    store(jz, zc - 1, t, j, flux_of(a[0], b[0], b))
                    if ring is not None:
                        fy[t][j] = flux_of(a[1], b[1], b)
                        fx[t][j] = flux_of(a[2], b[2], b)
                if d is not None:
                    v = (ez[t][j], ey[t][j], ex[t][j])
                    k = tangent(*a, *v, b)
                    store(gz, zc - 1, t, j, turn(a[0], b[0], v[0], k))
                    if ring is not None:
                        hy[t][j] = turn(a[1], b[1], v[1], k)
                        hx[t][j] = turn(a[2], b[2], v[2], k)
        if ring is None:
            return
        eb = [end_basis(ends(r)) for r in c]
        if with_flux:
            rows = halo_rows(ring_j, None, ring)
            out = cross(fx, fy, [end_flux(b) for b in eb], *rows)
            for t in range(T):
                for j in range(C):
                    store(jxy, ring, t, j, out[t][j])
        if d is not None:
            rows = halo_rows(ring_g, None, ring)
            out = cross(hx, hy, [end_tangent(b, ends(r)) for b, r in zip(eb, e)], *rows)
            for t in range(T):
                for j in range(C):
                    store(gxy, ring, t, j, out[t][j])

    def flux_ring(p_args, d_args=None, with_flux=True):
        for s in (0, 1):
            dz, dy, dx = ring_diffs(*p_args, s)
            if d_args is not None:
                ez, ey, ex = ring_diffs(*d_args, s)
            for j in range(C):
                b = basis(dz[j], dy[j], dx[j])
                if with_flux:
                    ring_j[s, :, block(j)] = flux_of(dy[j], b[1], b)
                if d_args is not None:
                    k = tangent(dz[j], dy[j], dx[j], ez[j], ey[j], ex[j], b)
                    ring_g[s, :, block(j)] = turn(dy[j], b[1], ey[j], k)

    def divergence(fz, fxy, z, t, j):
        at = (pl.ds(8 * t, 8), block(j))
        return 0.25 * ((fz[(z + 2, *at)] - fz[(z, *at)]) + fxy[(z, *at)])

    def laplacian(buf, zc, lo, hi):
        c, below, above = layer(buf, zc), layer(buf, zc - 1), layer(buf, zc + 1)
        down, up = shift_y(c, lo, hi)
        out = blank()
        for t in range(T):
            l, h = shift_x(c[t])
            for j in range(C):
                total = (below[t][j] + above[t][j]) + (down[t][j] + up[t][j])
                out[t][j] = c[t][j] + TIME_STEP * (total + (l[j] + h[j]) - 6.0 * c[t][j])
        return out

    def reaction(p, u):
        x = DRIVE_SHARP * (MELT_POINT - u)
        m = DRIVE_SCALE / math.pi * arctan(x)
        well = p * (1.0 - p)
        tilt = p - 0.5 + m
        slope = (-DRIVE_SHARP * DRIVE_SCALE / math.pi) * recip(1.0 + x * x)
        return well * tilt, (1.0 - 2.0 * p) * tilt + well, well * slope

    def over(lo, hi, body, step=1):
        def one_layer(i, carry):
            body(lo + i * step)
            return carry
        lax.fori_loop(0, (hi - lo + step - 1) // step, one_layer, 0)

    def inner(body):
        over(1, Z - 1, body)

    def outer(body):
        over(0, Z, body, Z - 1)

    def per_tile(body):
        def whole(z):
            for t in range(T):
                for j in range(C):
                    body(z, t, j)
        return whole

    def get(buf, z, t, j):
        return buf[z, pl.ds(8 * t, 8), block(j)]

    m_p0, m_y0, m_c0 = thick(p0), along_y(sy0, ry0), corners(sc0, rc0)
    m_u0, m_d1, m_t1 = thin(u0), thick(d1), thin(t1)
    m_y1, m_c1 = along_y(sy1, ry1), corners(sc1, rc1)
    m_p1, m_y2, m_c2 = thick(p1), along_y(sy2, ry2), corners(sc2, rc2)
    m_d0, m_t0 = thick(d0), thin(t0)
    m_y3, m_c3 = along_y(sy3, ry3), corners(sc3, rc3)

    @pl.when(zi == 0)
    def _():
        for buf in (p0, p1, d1, d0):
            buf[pl.ds(0, 2)] = jnp.zeros((2,) + buf.shape[1:], jnp.float32)
        for buf in (u0, t1, t0):
            buf[0] = jnp.zeros(buf.shape[1:], jnp.float32)

    @pl.when(zi == nz - 1)
    def _():
        for buf in (p0, p1, d1, d0):
            buf[pl.ds(Z + 2, 2)] = jnp.zeros((2,) + buf.shape[1:], jnp.float32)
        for buf in (u0, t1, t0):
            buf[Z + 1] = jnp.zeros(buf.shape[1:], jnp.float32)

    for s, at_end in ((0, yi == 0), (1, yi == ny - 1)):
        @pl.when(at_end)
        def _(s=s):
            for buf in (ry0, ry1, ry2, ry3):
                buf[s] = jnp.zeros(buf.shape[1:], jnp.float32)

    for i, side in enumerate(SIDES[4:]):
        @pl.when(jnp.logical_not(there(opposite(side))))
        def _(i=i):
            for buf in (rc0, rc1, rc2, rc3):
                buf[i] = jnp.zeros(buf.shape[1:], jnp.float32)

    def one(cond):
        return jnp.where(cond, 1, 0)

    local[0].wait()
    pack(p0, 2, 2, sy0, 0)
    pack_corner(p0, sc0)
    near_z = one(zi > 0) + one(zi < nz - 1)
    near_y = one(yi > 0) + one(yi < ny - 1)
    pl.semaphore_wait(barrier, near_z + near_y + near_z * near_y)
    start(m_y0 + m_c0 + m_p0)

    for copy in local[1:]:
        copy.wait()

    @per_tile
    def weight(z, t, j):
        w = get(sb, z, t, j) + LATENT_HEAT * get(t1, z + 1, t, j)
        store(d1, z + 2, t, j, TIME_STEP * get(kb, z, t, j) * w)
    over(0, Z, weight)
    pack(u0, 1, 1, sy1, 0)
    pack(d1, 2, 2, sy1, 1)
    pack(t1, 1, 1, sy1, 3)
    pack_corner(d1, sc1)
    start(m_y1 + m_c1 + m_u0 + m_d1 + m_t1)

    @per_tile
    def first_terms(z, t, j):
        a, b, c = reaction(get(p0, z + 2, t, j), get(u0, z + 1, t, j))
        store(r0, z, t, j, a)
        store(rp0, z, t, j, b)
        store(ru0, z, t, j, c)
    over(0, Z, first_terms)

    arrive(m_y0 + m_c0)
    flux_ring((ry0, 0, sy0, 0, rc0, 0))

    def flux0(z):
        flux_layer(p0, z + 2, halo_rows(ry0, 0, z), ring=z)
    inner(flux0)
    arrive(m_p0)
    outer(flux0)
    flux_layer(p0, 1, corner_rows(rc0, 0, True))
    flux_layer(p0, Z + 2, corner_rows(rc0, 0, False))

    @per_tile
    def advance(z, t, j):
        growth = divergence(jz, jxy, z, t, j) + get(r0, z, t, j)
        store(gr0, z, t, j, growth)
        gain = TIME_STEP * get(kb, z, t, j) * growth
        store(p1, z + 2, t, j, get(p0, z + 2, t, j) + gain)
    over(0, 2, advance)
    over(Z - 2, Z, advance)
    pack_corner(p1, sc2)
    start(m_c2 + m_p1)
    over(2, Z - 2, advance)
    pack(p1, 2, 2, sy2, 0)
    start(m_y2)

    arrive(m_y1 + m_c1 + m_u0 + m_d1 + m_t1)

    def second_terms(z):
        new_u = laplacian(u0, z + 1, *halo_rows(ry1, 0, z))
        new_t = laplacian(t1, z + 1, *halo_rows(ry1, 3, z))
        for t in range(T):
            for j in range(C):
                p = get(p1, z + 2, t, j)
                u = new_u[t][j] + LATENT_HEAT * (p - get(p0, z + 2, t, j))
                a, b, c = reaction(p, u)
                store(r1, z, t, j, a)
                store(rp1, z, t, j, b)
                store(ru1, z, t, j, c)
                store(tl1, z, t, j, new_t[t][j])
    over(0, Z, second_terms)

    arrive(m_y2 + m_c2)
    flux_ring((ry2, 0, sy2, 0, rc2, 0), (ry1, 1, sy1, 1, rc1, 0))

    def adjoint1(z):
        flux_layer(p1, z + 2, halo_rows(ry2, 0, z), d1, halo_rows(ry1, 1, z), ring=z)
    inner(adjoint1)
    arrive(m_p1)
    outer(adjoint1)
    flux_layer(p1, 1, corner_rows(rc2, 0, True), d1, corner_rows(rc1, 0, True))
    flux_layer(p1, Z + 2, corner_rows(rc2, 0, False), d1, corner_rows(rc1, 0, False))

    @per_tile
    def middle(z, t, j):
        d = get(d1, z + 2, t, j)
        pb = get(sb, z, t, j) + d * get(rp1, z, t, j) + divergence(gz, gxy, z, t, j)
        ub = get(tl1, z, t, j) + d * get(ru1, z, t, j)
        store(pb0, z, t, j, pb)
        store(t0, z + 1, t, j, ub)
        store(d0, z + 2, t, j, TIME_STEP * get(kb, z, t, j) * (pb + LATENT_HEAT * ub))
    over(0, 2, middle)
    over(Z - 2, Z, middle)
    pack_corner(d0, sc3)
    start(m_c3 + m_d0 + m_t0)
    over(2, Z - 2, middle)
    pack(d0, 2, 2, sy3, 0)
    pack(t0, 1, 1, sy3, 2)
    start(m_y3)

    @per_tile
    def mobility(z, t, j):
        growth = divergence(jz, jxy, z, t, j) + get(r1, z, t, j)
        late = get(sb, z, t, j) + LATENT_HEAT * get(t1, z + 1, t, j)
        early = get(pb0, z, t, j) + LATENT_HEAT * get(t0, z + 1, t, j)
        store(gm_out, z, t, j, TIME_STEP * (late * growth + early * get(gr0, z, t, j)))
    over(0, Z, mobility)

    arrive(m_y3 + m_c3)
    flux_ring((ry0, 0, sy0, 0, rc0, 0), (ry3, 0, sy3, 0, rc3, 0), False)

    def adjoint0(z):
        flux_layer(p0, z + 2, halo_rows(ry0, 0, z), d0, halo_rows(ry3, 0, z), False, ring=z)
    inner(adjoint0)
    arrive(m_d0 + m_t0)
    outer(adjoint0)
    flux_layer(p0, 1, corner_rows(rc0, 0, True), d0, corner_rows(rc3, 0, True), False)
    flux_layer(p0, Z + 2, corner_rows(rc0, 0, False), d0, corner_rows(rc3, 0, False), False)

    def finish(z):
        new_t = laplacian(t0, z + 1, *halo_rows(ry3, 2, z))
        for t in range(T):
            for j in range(C):
                d = get(d0, z + 2, t, j)
                pb = get(pb0, z, t, j) + d * get(rp0, z, t, j)
                store(sp_out, z, t, j, pb + divergence(gz, gxy, z, t, j))
                store(st_out, z, t, j, new_t[t][j] + d * get(ru0, z, t, j))
    over(0, Z, finish)

    sent(m_p0 + m_y0 + m_c0 + m_u0 + m_d1 + m_t1 + m_y1 + m_c1)
    sent(m_p1 + m_y2 + m_c2 + m_d0 + m_t0 + m_y3 + m_c3)


def body(nz, ny, *blocks):
    Z, Y, X = blocks[0].shape

    def buf(*shape):
        return pltpu.VMEM(shape, jnp.float32)

    thick, thin, flat = (Z + 4, Y, X), (Z + 2, Y, X), (Z, Y, X)
    scratch = [buf(*thick)] * 4 + [buf(*thin)] * 3 + [buf(*flat)] * 3
    scratch += [buf(*thin), buf(*flat)] * 2
    scratch += [buf(*flat)] * 9
    scratch += [buf(2, Z, X)] * 2
    scratch += [buf(2, n, Z, X) for n in (2, 2, 4, 4, 2, 2, 3, 3)]
    scratch += [buf(4, 1, 1, X)] * 8
    count = 38
    scratch += [pltpu.SemaphoreType.DMA((count,))] * 2 + [pltpu.SemaphoreType.DMA((5,))]
    vmem = pl.BlockSpec(memory_space=pltpu.VMEM)
    hbm = pl.BlockSpec(memory_space=pltpu.HBM)
    out = jax.ShapeDtypeStruct((Z, Y, X), jnp.float32)
    return pl.pallas_call(
        functools.partial(kernel, nz, ny),
        out_shape=(out, out, out),
        in_specs=[hbm] * 5,
        out_specs=(vmem, vmem, vmem),
        scratch_shapes=scratch,
        compiler_params=pltpu.CompilerParams(
            collective_id=0, has_side_effects=True, vmem_limit_bytes=40 * 1024 * 1024
        ),
    )(*blocks)


def solution(mesh):
    spec = P("gz", "gy", None)
    return jax.shard_map(
        functools.partial(body, mesh.shape["gz"], mesh.shape["gy"]),
        mesh=mesh,
        in_specs=(spec,) * 5,
        out_specs=(spec,) * 3,
        check_vma=False,
    )
```

time: 31.5 us -> 28.1 us (0.89)
  the two profiles are of different devices: /device:TPU:9 before, /device:TPU:0 now
where the time goes in v2:
time: 28.1 us; the launch traced here: 27.9 us
  Pallas kernels  20.4 us (73%)
  local copies, waits for them, and re-layouts  6.85 us (24%)
  between operations  0.65 us (2%)
    pallas_call x1, Pallas kernels, body(): pl.pallas_call(functools.partial(kernel, nz, ny), out_shape=(out, out, ou...  20.4 us
    unnamed x13, local copies, waits for them, and re-layouts  6.85 us

profile of v2, /device:TPU:0, one launch (start us, length us, event | category | flops | bytes accessed | tf_op | source)
XLA Modules:
  0.0 27.9 jit_solution(9475504638096942941)
XLA Ops:
  0.6 0.0 copy-start
  0.6 0.9 %copy-done = f32[8,16,512]{2,1,0:T(8,128)S(1)} copy-done((f32[8,16,512]{2,1,0:T(8,128)S(1)}, f32[8,16,512]{2,1,0:T(8,128)}, u32[]{:S(2)}) %copy-start) | copy-done | bytes 262168
  1.6 0.0 copy-start.1
  1.6 0.9 %copy-done.1 = f32[8,16,512]{2,1,0:T(8,128)S(1)} copy-done((f32[8,16,512]{2,1,0:T(8,128)S(1)}, f32[8,16,512]{2,1,0:T(8,128)}, u32[]{:S(2)}) %copy-start.1) | copy-done | bytes 262168
  2.5 0.0 copy-start.2
  2.5 0.9 %copy-done.2 = f32[8,16,512]{2,1,0:T(8,128)S(1)} copy-done((f32[8,16,512]{2,1,0:T(8,128)S(1)}, f32[8,16,512]{2,1,0:T(8,128)}, u32[]{:S(2)}) %copy-start.2) | copy-done | bytes 262168
  3.5 0.0 copy-start.3
  3.5 0.9 %copy-done.3 = f32[8,16,512]{2,1,0:T(8,128)S(1)} copy-done((f32[8,16,512]{2,1,0:T(8,128)S(1)}, f32[8,16,512]{2,1,0:T(8,128)}, u32[]{:S(2)}) %copy-start.3) | copy-done | bytes 262168
  4.4 0.0 copy-start.4
  4.4 0.9 %copy-done.4 = f32[8,16,512]{2,1,0:T(8,128)S(1)} copy-done((f32[8,16,512]{2,1,0:T(8,128)S(1)}, f32[8,16,512]{2,1,0:T(8,128)}, u32[]{:S(2)}) %copy-start.4) | copy-done | bytes 262168
  5.4 20.4 %shard_map.76 = (f32[8,16,512]{2,1,0:T(8,128)S(1)}, f32[8,16,512]{2,1,0:T(8,128)S(1)}, f32[8,16,512]{2,1,0:T(8,128)S(1)}) custom-call(f32[8,16,512]{2,1,0:T(8,128)S(1)} %copy-done, f32[8,16,512]{2,1,0:T(8,128)S(1)} %copy-done.1, f32[8,16,512]{2,1,0:T(8,128)S(1)} %copy-done.2, f32[8,16,512]{2,1,0:T(8,128)S(1)} %copy-done.3, f32[8,16,512]{2,1,0:T(8,128)S(1)} %copy-done.4), custom_call_target="tpu_custom_call" | custom-call | tf_op jit(solution)/shard_map/pallas_call | solution.py:599
  25.8 0.7 %copy.11 = f32[8,16,512]{2,1,0:T(8,128)} copy(f32[8,16,512]{2,1,0:T(8,128)S(1)} %get-tuple-element.6) | data formatting | bytes 524288
  26.5 0.7 %copy.12 = f32[8,16,512]{2,1,0:T(8,128)} copy(f32[8,16,512]{2,1,0:T(8,128)S(1)} %get-tuple-element.7) | data formatting | bytes 524288
  27.2 0.7 %copy.13 = f32[8,16,512]{2,1,0:T(8,128)} copy(f32[8,16,512]{2,1,0:T(8,128)S(1)} %get-tuple-element.8) | data formatting | bytes 524288
Async XLA Ops:
  0.6 1.0 %copy-start = (f32[8,16,512]{2,1,0:T(8,128)S(1)}, f32[8,16,512]{2,1,0:T(8,128)}, u32[]{:S(2)}) copy-start(f32[8,16,512]{2,1,0:T(8,128)} %p_in.1) | copy-start | bytes 786436
  1.6 0.9 %copy-start.1 = (f32[8,16,512]{2,1,0:T(8,128)S(1)}, f32[8,16,512]{2,1,0:T(8,128)}, u32[]{:S(2)}) copy-start(f32[8,16,512]{2,1,0:T(8,128)} %u_in.1) | copy-start | bytes 786436
  2.5 0.9 %copy-start.2 = (f32[8,16,512]{2,1,0:T(8,128)S(1)}, f32[8,16,512]{2,1,0:T(8,128)}, u32[]{:S(2)}) copy-start(f32[8,16,512]{2,1,0:T(8,128)} %k_in.1) | copy-start | bytes 786436
  3.5 0.9 %copy-start.3 = (f32[8,16,512]{2,1,0:T(8,128)S(1)}, f32[8,16,512]{2,1,0:T(8,128)}, u32[]{:S(2)}) copy-start(f32[8,16,512]{2,1,0:T(8,128)} %ps_in.1) | copy-start | bytes 786436
  4.4 0.9 %copy-start.4 = (f32[8,16,512]{2,1,0:T(8,128)S(1)}, f32[8,16,512]{2,1,0:T(8,128)}, u32[]{:S(2)}) copy-start(f32[8,16,512]{2,1,0:T(8,128)} %ts_in.1) | copy-start | bytes 786436

commit v3 on v2

--- a/solution.py
+++ b/solution.py
@@ -86,6 +86,7 @@
 def kernel(
     nz, ny,
     p_in, u_in, k_in, ps_in, ts_in,
+    sp_hbm, st_hbm, gm_hbm,
     sp_out, st_out, gm_out,
     p0, p1, d1, d0, u0, t1, t0, u1, kb, sb,
     jz, jxy, gz, gxy,
@@ -238,7 +239,10 @@
 
     def halo_rows(rim, at, z):
         at = () if at is None else (at,)
-        lo = [pltpu.roll(rim[(0, *at, slice(None), block(j))], lax.rem(Z - z, 8), 0) for j in range(C)]
+        if isinstance(z, int):
+            return wide_row(rim, 0, *at, z), wide_row(rim, 1, *at, z)
+        down = lax.rem(Z - z, 8)
+        lo = [pltpu.roll(rim[(0, *at, slice(None), block(j))], down, 0) for j in range(C)]
         hi = [pltpu.roll(rim[(1, *at, slice(None), block(j))], 7 - z, 0) for j in range(C)]
         return lo, hi
 
@@ -388,17 +392,26 @@
         slope = (-DRIVE_SHARP * DRIVE_SCALE / math.pi) * recip(1.0 + x * x)
         return well * tilt, (1.0 - 2.0 * p) * tilt + well, well * slope
 
-    def over(lo, hi, body, step=1):
-        def one_layer(i, carry):
-            body(lo + i * step)
+    def over(lo, hi, body, unroll=4):
+        if hi - lo <= unroll:
+            for z in range(lo, hi):
+                body(z)
+            return
+
+        def some_layers(i, carry):
+            for k in range(unroll):
+                body(lo + i * unroll + k)
             return carry
-        lax.fori_loop(0, (hi - lo + step - 1) // step, one_layer, 0)
+        lax.fori_loop(0, (hi - lo) // unroll, some_layers, 0)
+        for z in range(hi - (hi - lo) % unroll, hi):
+            body(z)
 
     def inner(body):
-        over(1, Z - 1, body)
+        over(1, Z - 1, body, 3)
 
     def outer(body):
-        over(0, Z, body, Z - 1)
+        body(0)
+        body(Z - 1)
 
     def per_tile(body):
         def whole(z):
@@ -493,8 +506,8 @@
         store(gr0, z, t, j, growth)
         gain = TIME_STEP * get(kb, z, t, j) * growth
         store(p1, z + 2, t, j, get(p0, z + 2, t, j) + gain)
-    over(0, 2, advance)
-    over(Z - 2, Z, advance)
+    for z in (0, 1, Z - 2, Z - 1):
+        advance(z)
     pack_corner(p1, sc2)
     start(m_c2 + m_p1)
     over(2, Z - 2, advance)
@@ -515,7 +528,7 @@
                 store(rp1, z, t, j, b)
                 store(ru1, z, t, j, c)
                 store(tl1, z, t, j, new_t[t][j])
-    over(0, Z, second_terms)
+    over(0, Z, second_terms, 2)
 
     arrive(m_y2 + m_c2)
     flux_ring((ry2, 0, sy2, 0, rc2, 0), (ry1, 1, sy1, 1, rc1, 0))
@@ -536,8 +549,8 @@
         store(pb0, z, t, j, pb)
         store(t0, z + 1, t, j, ub)
         store(d0, z + 2, t, j, TIME_STEP * get(kb, z, t, j) * (pb + LATENT_HEAT * ub))
-    over(0, 2, middle)
-    over(Z - 2, Z, middle)
+    for z in (0, 1, Z - 2, Z - 1):
+        middle(z)
     pack_corner(d0, sc3)
     start(m_c3 + m_d0 + m_t0)
     over(2, Z - 2, middle)
@@ -552,6 +565,8 @@
         early = get(pb0, z, t, j) + LATENT_HEAT * get(t0, z + 1, t, j)
         store(gm_out, z, t, j, TIME_STEP * (late * growth + early * get(gr0, z, t, j)))
     over(0, Z, mobility)
+    writes = [pltpu.make_async_copy(gm_out, gm_hbm, lsem.at[5])]
+    writes[0].start()
 
     arrive(m_y3 + m_c3)
     flux_ring((ry0, 0, sy0, 0, rc0, 0), (ry3, 0, sy3, 0, rc3, 0), False)
@@ -572,10 +587,18 @@
                 pb = get(pb0, z, t, j) + d * get(rp0, z, t, j)
                 store(sp_out, z, t, j, pb + divergence(gz, gxy, z, t, j))
                 store(st_out, z, t, j, new_t[t][j] + d * get(ru0, z, t, j))
-    over(0, Z, finish)
+    half = Z // 2
+    for i in (0, 1):
+        over(i * half, (i + 1) * half, finish, 2)
+        part = pl.ds(i * half, half)
+        for k, (src, dst) in enumerate(((sp_out, sp_hbm), (st_out, st_hbm))):
+            writes.append(pltpu.make_async_copy(src.at[part], dst.at[part], lsem.at[6 + 2 * i + k]))
+            writes[-1].start()
 
     sent(m_p0 + m_y0 + m_c0 + m_u0 + m_d1 + m_t1 + m_y1 + m_c1)
     sent(m_p1 + m_y2 + m_c2 + m_d0 + m_t0 + m_y3 + m_c3)
+    for copy in writes:
+        copy.wait()
 
 
 def body(nz, ny, *blocks):
@@ -585,25 +608,24 @@
         return pltpu.VMEM(shape, jnp.float32)
 
     thick, thin, flat = (Z + 4, Y, X), (Z + 2, Y, X), (Z, Y, X)
-    scratch = [buf(*thick)] * 4 + [buf(*thin)] * 3 + [buf(*flat)] * 3
+    scratch = [buf(*flat)] * 3 + [buf(*thick)] * 4 + [buf(*thin)] * 3 + [buf(*flat)] * 3
     scratch += [buf(*thin), buf(*flat)] * 2
     scratch += [buf(*flat)] * 9
     scratch += [buf(2, Z, X)] * 2
     scratch += [buf(2, n, Z, X) for n in (2, 2, 4, 4, 2, 2, 3, 3)]
     scratch += [buf(4, 1, 1, X)] * 8
     count = 38
-    scratch += [pltpu.SemaphoreType.DMA((count,))] * 2 + [pltpu.SemaphoreType.DMA((5,))]
-    vmem = pl.BlockSpec(memory_space=pltpu.VMEM)
+    scratch += [pltpu.SemaphoreType.DMA((count,))] * 2 + [pltpu.SemaphoreType.DMA((10,))]
     hbm = pl.BlockSpec(memory_space=pltpu.HBM)
     out = jax.ShapeDtypeStruct((Z, Y, X), jnp.float32)
     return pl.pallas_call(
         functools.partial(kernel, nz, ny),
         out_shape=(out, out, out),
         in_specs=[hbm] * 5,
-        out_specs=(vmem, vmem, vmem),
+        out_specs=(hbm, hbm, hbm),
         scratch_shapes=scratch,
         compiler_params=pltpu.CompilerParams(
-            collective_id=0, has_side_effects=True, vmem_limit_bytes=40 * 1024 * 1024
+            collective_id=0, has_side_effects=True, vmem_limit_bytes=62 * 1024 * 1024
         ),
     )(*blocks)
 

time: 28.1 us -> 22.9 us (0.81)
  the two profiles are of different devices: /device:TPU:0 before, /device:TPU:9 now
where the time goes in v3:
time: 22.9 us; the launch traced here: 22.4 us
  Pallas kernels  18.3 us (80%)
  local copies, waits for them, and re-layouts  3.46 us (15%)
  between operations  0.65 us (3%)
    pallas_call x1, Pallas kernels, body(): pl.pallas_call(functools.partial(kernel, nz, ny), out_shape=(out, out, ou...  18.3 us
    unnamed x7, local copies, waits for them, and re-layouts  3.46 us

profile of v3, /device:TPU:9, one launch (start us, length us, event | category | flops | bytes accessed | tf_op | source)
XLA Modules:
  0.0 22.4 jit_solution(8681513303619021346)
XLA Ops:
  0.6 18.3 %shard_map.76 = (f32[8,16,512]{2,1,0:T(8,128)}, f32[8,16,512]{2,1,0:T(8,128)}, f32[8,16,512]{2,1,0:T(8,128)}) custom-call(f32[8,16,512]{2,1,0:T(8,128)} %p_in.1, f32[8,16,512]{2,1,0:T(8,128)} %u_in.1, f32[8,16,512]{2,1,0:T(8,128)} %k_in.1, f32[8,16,512]{2,1,0:T(8,128)} %ps_in.1, f32[8,16,512]{2,1,0:T(8,128)} %ts_in.1), custom_call_target="tpu_custom_call" | custom-call | tf_op jit(solution)/shard_map/pallas_call | solution.py:621
  19.0 0.0 copy-start.1
  19.0 1.7 %copy.11 = f32[8,16,512]{2,1,0:T(8,128)} copy(f32[8,16,512]{2,1,0:T(8,128)} %get-tuple-element.6) | data formatting | bytes 524288
  20.7 0.0 copy-done.1
  20.7 0.0 copy-start
  20.7 0.7 %copy.12 = f32[8,16,512]{2,1,0:T(8,128)} copy(f32[8,16,512]{2,1,0:T(8,128)S(1)} %copy-done.1) | data formatting | bytes 524288
  21.4 0.3 %copy-done = f32[8,16,512]{2,1,0:T(8,128)S(1)} copy-done((f32[8,16,512]{2,1,0:T(8,128)S(1)}, f32[8,16,512]{2,1,0:T(8,128)}, u32[]{:S(2)}) %copy-start) | copy-done | bytes 262168
  21.7 0.7 %copy.13 = f32[8,16,512]{2,1,0:T(8,128)} copy(f32[8,16,512]{2,1,0:T(8,128)S(1)} %copy-done) | data formatting | bytes 524288
Async XLA Ops:
  19.0 1.7 %copy-start.1 = (f32[8,16,512]{2,1,0:T(8,128)S(1)}, f32[8,16,512]{2,1,0:T(8,128)}, u32[]{:S(2)}) copy-start(f32[8,16,512]{2,1,0:T(8,128)} %get-tuple-element.7) | copy-start | bytes 786436
  20.7 1.0 %copy-start = (f32[8,16,512]{2,1,0:T(8,128)S(1)}, f32[8,16,512]{2,1,0:T(8,128)}, u32[]{:S(2)}) copy-start(f32[8,16,512]{2,1,0:T(8,128)} %get-tuple-element.8) | copy-start | bytes 786436

commit v4 on v3

--- a/solution.py
+++ b/solution.py
@@ -123,17 +123,19 @@
     local = [
         pltpu.make_async_copy(src, dst, lsem.at[i])
         for i, (src, dst) in enumerate((
-            (p_in, p0.at[pl.ds(2, Z)]),
-            (k_in, kb),
             (ps_in, sb),
             (ts_in, t1.at[pl.ds(1, Z)]),
+            (k_in, kb),
+            (p_in, p0.at[pl.ds(2, Z)]),
             (u_in, u0.at[pl.ds(1, Z)]),
+            (p_in.at[:, 0], sy0.at[0, 0]),
+            (p_in.at[:, Y - 1], sy0.at[1, 0]),
         ))
     ]
     for copy in local:
         copy.start()
 
-    slots = iter(range(1000))
+    slots = iter(range(rsem.shape[0]))
 
     def message(side, src, dst):
         slot = next(slots)
@@ -167,10 +169,38 @@
             message((-1, 0), buf.at[pl.ds(1, 1)], buf.at[pl.ds(Z + 1, 1)]),
         ]
 
-    def along_y(src, dst):
+    def along_y(src, dst, at, deep=1):
+        part = pl.ds(at, deep)
         return [
-            message((0, 1), src.at[1], dst.at[0]),
-            message((0, -1), src.at[0], dst.at[1]),
+            message((0, 1), src.at[1, part], dst.at[0, part]),
+            message((0, -1), src.at[0, part], dst.at[1, part]),
+        ]
+
+    def thick_in(src, buf):
+        return [
+            message((1, 0), src.at[pl.ds(Z - 2, 2)], buf.at[pl.ds(0, 2)]),
+            message((-1, 0), src.at[pl.ds(0, 2)], buf.at[pl.ds(Z + 2, 2)]),
+        ]
+
+    def thin_in(src, buf):
+        return [
+            message((1, 0), src.at[pl.ds(Z - 1, 1)], buf.at[pl.ds(0, 1)]),
+            message((-1, 0), src.at[pl.ds(0, 1)], buf.at[pl.ds(Z + 1, 1)]),
+        ]
+
+    def row_in(src, y, dst, at):
+        return [
+            message((0, 1), src.at[:, Y - 1 - y], dst.at[0, at]),
+            message((0, -1), src.at[:, y], dst.at[1, at]),
+        ]
+
+    def corners_in(src, dst):
+        return [
+            message(
+                side, src.at[Z - 1 if side[0] > 0 else 0, Y - 1 if side[1] > 0 else 0],
+                dst.at[i, 0, 0],
+            )
+            for i, side in enumerate(SIDES[4:])
         ]
 
     def corners(src, dst):
@@ -269,8 +299,8 @@
         up = [jnp.where(bottom, hi[j], pltpu.roll(near[j], 7, 0)) for j in range(C)]
         return [down], [up]
 
-    def pack(src, base, deep, dst, at):
-        for k in range(deep):
+    def pack(src, base, deep, dst, at, skip=0):
+        for k in range(skip, deep):
             for s, y in ((0, k), (1, Y - 1 - k)):
                 total = wide_row(src, base, y)
                 for z in range(1, Z):
@@ -308,9 +338,9 @@
         d_b = r * (TWIST * RISE * dq - (2.0 * TWIST) * a * r * m)
         return (big_a + 3.0 * big_b * xx) * e + d * (d_a + d_b * xx)
 
-    def cross(fx, fy, end, lo, hi):
+    def cross(fx, fy, end):
         out = []
-        down, up = shift_y(fy, lo, hi)
+        down, up = shift_y(fy, [0.0] * C, [0.0] * C)
         for t in range(T):
             l, h = shift_x(fx[t], end[t])
             out.append([(h[j] - l[j]) + (up[t][j] - down[t][j]) for j in range(C)])
@@ -344,14 +374,12 @@
             return
         eb = [end_basis(ends(r)) for r in c]
         if with_flux:
-            rows = halo_rows(ring_j, None, ring)
-            out = cross(fx, fy, [end_flux(b) for b in eb], *rows)
+            out = cross(fx, fy, [end_flux(b) for b in eb])
             for t in range(T):
                 for j in range(C):
                     store(jxy, ring, t, j, out[t][j])
         if d is not None:
-            rows = halo_rows(ring_g, None, ring)
-            out = cross(hx, hy, [end_tangent(b, ends(r)) for b, r in zip(eb, e)], *rows)
+            out = cross(hx, hy, [end_tangent(b, ends(r)) for b, r in zip(eb, e)])
             for t in range(T):
                 for j in range(C):
                     store(gxy, ring, t, j, out[t][j])
@@ -369,9 +397,19 @@
                     k = tangent(dz[j], dy[j], dx[j], ez[j], ey[j], ex[j], b)
                     ring_g[s, :, block(j)] = turn(dy[j], b[1], ey[j], k)
 
-    def divergence(fz, fxy, z, t, j):
-        at = (pl.ds(8 * t, 8), block(j))
-        return 0.25 * ((fz[(z + 2, *at)] - fz[(z, *at)]) + fxy[(z, *at)])
+    def divergence(fz, fxy, ring, z):
+        lo, hi = halo_rows(ring, None, z)
+        out = blank()
+        for t in range(T):
+            for j in range(C):
+                at = (pl.ds(8 * t, 8), block(j))
+                total = (fz[(z + 2, *at)] - fz[(z, *at)]) + fxy[(z, *at)]
+                if t == 0:
+                    total = jnp.where(top, total - lo[j], total)
+                if t == T - 1:
+                    total = jnp.where(bottom, total + hi[j], total)
+                out[t][j] = 0.25 * total
+        return out
 
     def laplacian(buf, zc, lo, hi):
         c, below, above = layer(buf, zc), layer(buf, zc - 1), layer(buf, zc + 1)
@@ -420,15 +458,26 @@
                     body(z, t, j)
         return whole
 
+    def with_divergence(fz, fxy, ring, body):
+        def whole(z):
+            div = divergence(fz, fxy, ring, z)
+            for t in range(T):
+                for j in range(C):
+                    body(z, t, j, div[t][j])
+        return whole
+
     def get(buf, z, t, j):
         return buf[z, pl.ds(8 * t, 8), block(j)]
 
-    m_p0, m_y0, m_c0 = thick(p0), along_y(sy0, ry0), corners(sc0, rc0)
-    m_u0, m_d1, m_t1 = thin(u0), thick(d1), thin(t1)
-    m_y1, m_c1 = along_y(sy1, ry1), corners(sc1, rc1)
-    m_p1, m_y2, m_c2 = thick(p1), along_y(sy2, ry2), corners(sc2, rc2)
-    m_d0, m_t0 = thick(d0), thin(t0)
-    m_y3, m_c3 = along_y(sy3, ry3), corners(sc3, rc3)
+    m_y0, m_p0 = row_in(p_in, 0, ry0, 0), thick_in(p_in, p0)
+    m_f0, m_c0 = row_in(p_in, 1, ry0, 1), corners_in(p_in, rc0)
+    m_d1, m_y1, m_c1 = thick(d1), along_y(sy1, ry1, 1, 2), corners(sc1, rc1)
+    m_ut = thin_in(u_in, u0) + thin_in(ts_in, t1)
+    m_ut += row_in(u_in, 0, ry1, 0) + row_in(ts_in, 0, ry1, 3)
+    m_y2, m_p1 = along_y(sy2, ry2, 0), thick(p1)
+    m_f2, m_c2 = along_y(sy2, ry2, 1), corners(sc2, rc2)
+    m_y3, m_d0, m_t0 = along_y(sy3, ry3, 0), thick(d0), thin(t0)
+    m_f3, m_c3 = along_y(sy3, ry3, 1, 2), corners(sc3, rc3)
 
     @pl.when(zi == 0)
     def _():
@@ -459,15 +508,12 @@
     def one(cond):
         return jnp.where(cond, 1, 0)
 
-    local[0].wait()
-    pack(p0, 2, 2, sy0, 0)
-    pack_corner(p0, sc0)
     near_z = one(zi > 0) + one(zi < nz - 1)
     near_y = one(yi > 0) + one(yi < ny - 1)
     pl.semaphore_wait(barrier, near_z + near_y + near_z * near_y)
-    start(m_y0 + m_c0 + m_p0)
-
-    for copy in local[1:]:
+    start(m_y0 + m_p0 + m_f0 + m_c0)
+
+    for copy in local[:3]:
         copy.wait()
 
     @per_tile
@@ -475,11 +521,11 @@
         w = get(sb, z, t, j) + LATENT_HEAT * get(t1, z + 1, t, j)
         store(d1, z + 2, t, j, TIME_STEP * get(kb, z, t, j) * w)
     over(0, Z, weight)
-    pack(u0, 1, 1, sy1, 0)
     pack(d1, 2, 2, sy1, 1)
-    pack(t1, 1, 1, sy1, 3)
     pack_corner(d1, sc1)
-    start(m_y1 + m_c1 + m_u0 + m_d1 + m_t1)
+    start(m_d1 + m_y1 + m_c1 + m_ut)
+    for copy in local[3:]:
+        copy.wait()
 
     @per_tile
     def first_terms(z, t, j):
@@ -489,32 +535,32 @@
         store(ru0, z, t, j, c)
     over(0, Z, first_terms)
 
-    arrive(m_y0 + m_c0)
-    flux_ring((ry0, 0, sy0, 0, rc0, 0))
-
     def flux0(z):
         flux_layer(p0, z + 2, halo_rows(ry0, 0, z), ring=z)
+    arrive(m_y0)
     inner(flux0)
+    arrive(m_f0 + m_c0)
+    flux_ring((ry0, 0, sy0, 0, rc0, 0))
     arrive(m_p0)
     outer(flux0)
     flux_layer(p0, 1, corner_rows(rc0, 0, True))
     flux_layer(p0, Z + 2, corner_rows(rc0, 0, False))
 
-    @per_tile
-    def advance(z, t, j):
-        growth = divergence(jz, jxy, z, t, j) + get(r0, z, t, j)
+    def advance_cell(z, t, j, div):
+        growth = div + get(r0, z, t, j)
         store(gr0, z, t, j, growth)
         gain = TIME_STEP * get(kb, z, t, j) * growth
         store(p1, z + 2, t, j, get(p0, z + 2, t, j) + gain)
-    for z in (0, 1, Z - 2, Z - 1):
-        advance(z)
+    advance = with_divergence(jz, jxy, ring_j, advance_cell)
+    over(0, Z, advance)
+    pack(p1, 2, 1, sy2, 0)
+    start(m_y2 + m_p1)
     pack_corner(p1, sc2)
-    start(m_c2 + m_p1)
-    over(2, Z - 2, advance)
-    pack(p1, 2, 2, sy2, 0)
-    start(m_y2)
-
-    arrive(m_y1 + m_c1 + m_u0 + m_d1 + m_t1)
+    start(m_c2)
+    pack(p1, 2, 2, sy2, 0, 1)
+    start(m_f2)
+
+    arrive(m_ut)
 
     def second_terms(z):
         new_u = laplacian(u0, z + 1, *halo_rows(ry1, 0, z))
@@ -530,50 +576,50 @@
                 store(tl1, z, t, j, new_t[t][j])
     over(0, Z, second_terms, 2)
 
-    arrive(m_y2 + m_c2)
-    flux_ring((ry2, 0, sy2, 0, rc2, 0), (ry1, 1, sy1, 1, rc1, 0))
-
     def adjoint1(z):
         flux_layer(p1, z + 2, halo_rows(ry2, 0, z), d1, halo_rows(ry1, 1, z), ring=z)
+    arrive(m_y1 + m_c1 + m_d1 + m_y2)
     inner(adjoint1)
+    arrive(m_f2 + m_c2)
+    flux_ring((ry2, 0, sy2, 0, rc2, 0), (ry1, 1, sy1, 1, rc1, 0))
     arrive(m_p1)
     outer(adjoint1)
     flux_layer(p1, 1, corner_rows(rc2, 0, True), d1, corner_rows(rc1, 0, True))
     flux_layer(p1, Z + 2, corner_rows(rc2, 0, False), d1, corner_rows(rc1, 0, False))
 
-    @per_tile
-    def middle(z, t, j):
+    def middle_cell(z, t, j, div):
         d = get(d1, z + 2, t, j)
-        pb = get(sb, z, t, j) + d * get(rp1, z, t, j) + divergence(gz, gxy, z, t, j)
+        pb = get(sb, z, t, j) + d * get(rp1, z, t, j) + div
         ub = get(tl1, z, t, j) + d * get(ru1, z, t, j)
         store(pb0, z, t, j, pb)
         store(t0, z + 1, t, j, ub)
         store(d0, z + 2, t, j, TIME_STEP * get(kb, z, t, j) * (pb + LATENT_HEAT * ub))
-    for z in (0, 1, Z - 2, Z - 1):
-        middle(z)
+    middle = with_divergence(gz, gxy, ring_g, middle_cell)
+    over(0, Z, middle)
+    pack(d0, 2, 1, sy3, 0)
+    start(m_y3 + m_d0)
     pack_corner(d0, sc3)
-    start(m_c3 + m_d0 + m_t0)
-    over(2, Z - 2, middle)
-    pack(d0, 2, 2, sy3, 0)
+    start(m_c3)
+    pack(d0, 2, 2, sy3, 0, 1)
     pack(t0, 1, 1, sy3, 2)
-    start(m_y3)
-
-    @per_tile
-    def mobility(z, t, j):
-        growth = divergence(jz, jxy, z, t, j) + get(r1, z, t, j)
+    start(m_f3 + m_t0)
+
+    def mobility_cell(z, t, j, div):
+        growth = div + get(r1, z, t, j)
         late = get(sb, z, t, j) + LATENT_HEAT * get(t1, z + 1, t, j)
         early = get(pb0, z, t, j) + LATENT_HEAT * get(t0, z + 1, t, j)
         store(gm_out, z, t, j, TIME_STEP * (late * growth + early * get(gr0, z, t, j)))
+    mobility = with_divergence(jz, jxy, ring_j, mobility_cell)
     over(0, Z, mobility)
-    writes = [pltpu.make_async_copy(gm_out, gm_hbm, lsem.at[5])]
+    writes = [pltpu.make_async_copy(gm_out, gm_hbm, lsem.at[7])]
     writes[0].start()
-
-    arrive(m_y3 + m_c3)
-    flux_ring((ry0, 0, sy0, 0, rc0, 0), (ry3, 0, sy3, 0, rc3, 0), False)
 
     def adjoint0(z):
         flux_layer(p0, z + 2, halo_rows(ry0, 0, z), d0, halo_rows(ry3, 0, z), False, ring=z)
+    arrive(m_y3)
     inner(adjoint0)
+    arrive(m_f3 + m_c3)
+    flux_ring((ry0, 0, sy0, 0, rc0, 0), (ry3, 0, sy3, 0, rc3, 0), False)
     arrive(m_d0 + m_t0)
     outer(adjoint0)
     flux_layer(p0, 1, corner_rows(rc0, 0, True), d0, corner_rows(rc3, 0, True), False)
@@ -581,23 +627,37 @@
 
     def finish(z):
         new_t = laplacian(t0, z + 1, *halo_rows(ry3, 2, z))
+        div = divergence(gz, gxy, ring_g, z)
         for t in range(T):
             for j in range(C):
                 d = get(d0, z + 2, t, j)
                 pb = get(pb0, z, t, j) + d * get(rp0, z, t, j)
-                store(sp_out, z, t, j, pb + divergence(gz, gxy, z, t, j))
+                store(sp_out, z, t, j, pb + div[t][j])
                 store(st_out, z, t, j, new_t[t][j] + d * get(ru0, z, t, j))
     half = Z // 2
     for i in (0, 1):
         over(i * half, (i + 1) * half, finish, 2)
         part = pl.ds(i * half, half)
         for k, (src, dst) in enumerate(((sp_out, sp_hbm), (st_out, st_hbm))):
-            writes.append(pltpu.make_async_copy(src.at[part], dst.at[part], lsem.at[6 + 2 * i + k]))
+            writes.append(pltpu.make_async_copy(src.at[part], dst.at[part], lsem.at[8 + 2 * i + k]))
             writes[-1].start()
 
-    sent(m_p0 + m_y0 + m_c0 + m_u0 + m_d1 + m_t1 + m_y1 + m_c1)
-    sent(m_p1 + m_y2 + m_c2 + m_d0 + m_t0 + m_y3 + m_c3)
+    sent(m_y0 + m_p0 + m_f0 + m_c0 + m_d1 + m_y1 + m_c1 + m_ut)
+    sent(m_y2 + m_p1 + m_f2 + m_c2 + m_y3 + m_d0 + m_t0 + m_f3 + m_c3)
     for copy in writes:
+        copy.wait()
+
+
+def deliver(*refs):
+    ins, outs, sem = refs[:3], refs[3:6], refs[6]
+    Z = ins[0].shape[0]
+    copies = []
+    for src, dst in zip(ins, outs):
+        for z in range(0, Z, 2):
+            part = pl.ds(z, 2)
+            copies.append(pltpu.make_async_copy(src.at[part], dst.at[part], sem.at[len(copies)]))
+            copies[-1].start()
+    for copy in copies:
         copy.wait()
 
 
@@ -614,11 +674,11 @@
     scratch += [buf(2, Z, X)] * 2
     scratch += [buf(2, n, Z, X) for n in (2, 2, 4, 4, 2, 2, 3, 3)]
     scratch += [buf(4, 1, 1, X)] * 8
-    count = 38
-    scratch += [pltpu.SemaphoreType.DMA((count,))] * 2 + [pltpu.SemaphoreType.DMA((10,))]
+    count = 48
+    scratch += [pltpu.SemaphoreType.DMA((count,))] * 2 + [pltpu.SemaphoreType.DMA((12,))]
     hbm = pl.BlockSpec(memory_space=pltpu.HBM)
     out = jax.ShapeDtypeStruct((Z, Y, X), jnp.float32)
-    return pl.pallas_call(
+    results = pl.pallas_call(
         functools.partial(kernel, nz, ny),
         out_shape=(out, out, out),
         in_specs=[hbm] * 5,
@@ -628,6 +688,14 @@
             collective_id=0, has_side_effects=True, vmem_limit_bytes=62 * 1024 * 1024
         ),
     )(*blocks)
+    return pl.pallas_call(
+        deliver,
+        out_shape=(out, out, out),
+        in_specs=[hbm] * 3,
+        out_specs=(hbm, hbm, hbm),
+        scratch_shapes=[pltpu.SemaphoreType.DMA((3 * (Z // 2),))],
+        compiler_params=pltpu.CompilerParams(vmem_limit_bytes=62 * 1024 * 1024),
+    )(*results)
 
 
 def solution(mesh):

time: 22.9 us -> 45 us (1.97)
  Pallas kernels: 18.3 us -> 44.2 us
  local copies, waits for them, and re-layouts: 3.46 us -> 0 us
    pallas_call x0 -> x1, Pallas kernels: none -> 25 us  [body(): pl.pallas_call(deliver, out_shape=(out, out, out), in_specs=[hbm] * 3, ou...]
    unnamed x7 -> x0, local copies, waits for them, and re-layouts: 3.46 us -> none
    pallas_call x1, Pallas kernels: 18.3 us -> 19.2 us  [body(): pl.pallas_call(functools.partial(kernel, nz, ny), out_shape=(out, out, ou...]
where the time goes in v4:
time: 45 us; the launch traced here: 44.8 us
  Pallas kernels  44.2 us (98%)
  between operations  0.64 us (1%)
    pallas_call x1, Pallas kernels, body(): pl.pallas_call(deliver, out_shape=(out, out, out), in_specs=[hbm] * 3, ou...  25 us
    pallas_call x1, Pallas kernels, body(): pl.pallas_call(functools.partial(kernel, nz, ny), out_shape=(out, out, ou...  19.2 us

profile of v4, /device:TPU:9, one launch (start us, length us, event | category | flops | bytes accessed | tf_op | source)
XLA Modules:
  0.0 44.8 jit_solution(4916401300289031251)
XLA Ops:
  0.6 19.2 %shard_map.76 = (f32[8,16,512]{2,1,0:T(8,128)}, f32[8,16,512]{2,1,0:T(8,128)}, f32[8,16,512]{2,1,0:T(8,128)}) custom-call(f32[8,16,512]{2,1,0:T(8,128)} %p_in.1, f32[8,16,512]{2,1,0:T(8,128)} %u_in.1, f32[8,16,512]{2,1,0:T(8,128)} %k_in.1, f32[8,16,512]{2,1,0:T(8,128)} %ps_in.1, f32[8,16,512]{2,1,0:T(8,128)} %ts_in.1), custom_call_target="tpu_custom_call" | custom-call | tf_op jit(solution)/shard_map/pallas_call | solution.py:681
  19.8 25.0 %shard_map.77 = (f32[8,16,512]{2,1,0:T(8,128)}, f32[8,16,512]{2,1,0:T(8,128)}, f32[8,16,512]{2,1,0:T(8,128)}) custom-call(f32[8,16,512]{2,1,0:T(8,128)} %get-tuple-element.6.refs_0_, f32[8,16,512]{2,1,0:T(8,128)} %get-tuple-element.7.refs_1_, f32[8,16,512]{2,1,0:T(8,128)} %get-tuple-element.8.refs_2_), custom_call_target="tpu_custom_call" | custom-call | tf_op jit(solution)/shard_map/pallas_call | solution.py:691

commit v5 on v4

--- a/solution.py
+++ b/solution.py
@@ -86,7 +86,6 @@
 def kernel(
     nz, ny,
     p_in, u_in, k_in, ps_in, ts_in,
-    sp_hbm, st_hbm, gm_hbm,
     sp_out, st_out, gm_out,
     p0, p1, d1, d0, u0, t1, t0, u1, kb, sb,
     jz, jxy, gz, gxy,
@@ -122,15 +121,16 @@
 
     local = [
         pltpu.make_async_copy(src, dst, lsem.at[i])
-        for i, (src, dst) in enumerate((
-            (ps_in, sb),
-            (ts_in, t1.at[pl.ds(1, Z)]),
-            (k_in, kb),
-            (p_in, p0.at[pl.ds(2, Z)]),
-            (u_in, u0.at[pl.ds(1, Z)]),
-            (p_in.at[:, 0], sy0.at[0, 0]),
-            (p_in.at[:, Y - 1], sy0.at[1, 0]),
-        ))
+        for i, (src, dst) in enumerate(
+            [
+                (src.at[pl.ds(z, Z // 2)], dst.at[pl.ds(base + z, Z // 2)])
+                for src, dst, base in (
+                    (ps_in, sb, 0), (ts_in, t1, 1), (k_in, kb, 0), (p_in, p0, 2), (u_in, u0, 1)
+                )
+                for z in (0, Z // 2)
+            ]
+            + [(p_in.at[:, 0], sy0.at[0, 0]), (p_in.at[:, Y - 1], sy0.at[1, 0])]
+        )
     ]
     for copy in local:
         copy.start()
@@ -513,7 +513,7 @@
     pl.semaphore_wait(barrier, near_z + near_y + near_z * near_y)
     start(m_y0 + m_p0 + m_f0 + m_c0)
 
-    for copy in local[:3]:
+    for copy in local[:6]:
         copy.wait()
 
     @per_tile
@@ -524,7 +524,7 @@
     pack(d1, 2, 2, sy1, 1)
     pack_corner(d1, sc1)
     start(m_d1 + m_y1 + m_c1 + m_ut)
-    for copy in local[3:]:
+    for copy in local[6:]:
         copy.wait()
 
     @per_tile
@@ -611,8 +611,6 @@
         store(gm_out, z, t, j, TIME_STEP * (late * growth + early * get(gr0, z, t, j)))
     mobility = with_divergence(jz, jxy, ring_j, mobility_cell)
     over(0, Z, mobility)
-    writes = [pltpu.make_async_copy(gm_out, gm_hbm, lsem.at[7])]
-    writes[0].start()
 
     def adjoint0(z):
         flux_layer(p0, z + 2, halo_rows(ry0, 0, z), d0, halo_rows(ry3, 0, z), False, ring=z)
@@ -634,18 +632,9 @@
                 pb = get(pb0, z, t, j) + d * get(rp0, z, t, j)
                 store(sp_out, z, t, j, pb + div[t][j])
                 store(st_out, z, t, j, new_t[t][j] + d * get(ru0, z, t, j))
-    half = Z // 2
-    for i in (0, 1):
-        over(i * half, (i + 1) * half, finish, 2)
-        part = pl.ds(i * half, half)
-        for k, (src, dst) in enumerate(((sp_out, sp_hbm), (st_out, st_hbm))):
-            writes.append(pltpu.make_async_copy(src.at[part], dst.at[part], lsem.at[8 + 2 * i + k]))
-            writes[-1].start()
-
+    over(0, Z, finish, 2)
     sent(m_y0 + m_p0 + m_f0 + m_c0 + m_d1 + m_y1 + m_c1 + m_ut)
     sent(m_y2 + m_p1 + m_f2 + m_c2 + m_y3 + m_d0 + m_t0 + m_f3 + m_c3)
-    for copy in writes:
-        copy.wait()
 
 
 def deliver(*refs):
@@ -668,7 +657,7 @@
         return pltpu.VMEM(shape, jnp.float32)
 
     thick, thin, flat = (Z + 4, Y, X), (Z + 2, Y, X), (Z, Y, X)
-    scratch = [buf(*flat)] * 3 + [buf(*thick)] * 4 + [buf(*thin)] * 3 + [buf(*flat)] * 3
+    scratch = [buf(*thick)] * 4 + [buf(*thin)] * 3 + [buf(*flat)] * 3
     scratch += [buf(*thin), buf(*flat)] * 2
     scratch += [buf(*flat)] * 9
     scratch += [buf(2, Z, X)] * 2
@@ -677,12 +666,14 @@
     count = 48
     scratch += [pltpu.SemaphoreType.DMA((count,))] * 2 + [pltpu.SemaphoreType.DMA((12,))]
     hbm = pl.BlockSpec(memory_space=pltpu.HBM)
+    vmem = pl.BlockSpec(memory_space=pltpu.VMEM)
+    kept = pltpu.VMEM((Z, Y, X), jnp.float32)
     out = jax.ShapeDtypeStruct((Z, Y, X), jnp.float32)
     results = pl.pallas_call(
         functools.partial(kernel, nz, ny),
-        out_shape=(out, out, out),
+        out_shape=(kept, kept, kept),
         in_specs=[hbm] * 5,
-        out_specs=(hbm, hbm, hbm),
+        out_specs=(vmem, vmem, vmem),
         scratch_shapes=scratch,
         compiler_params=pltpu.CompilerParams(
             collective_id=0, has_side_effects=True, vmem_limit_bytes=62 * 1024 * 1024
@@ -691,10 +682,10 @@
     return pl.pallas_call(
         deliver,
         out_shape=(out, out, out),
-        in_specs=[hbm] * 3,
+        in_specs=[vmem] * 3,
         out_specs=(hbm, hbm, hbm),
         scratch_shapes=[pltpu.SemaphoreType.DMA((3 * (Z // 2),))],
-        compiler_params=pltpu.CompilerParams(vmem_limit_bytes=62 * 1024 * 1024),
+        compiler_params=pltpu.CompilerParams(vmem_limit_bytes=8 * 1024 * 1024),
     )(*results)
 
 

time: 45 us -> 20.3 us (0.45)
  Pallas kernels: 44.2 us -> 19.6 us
    pallas_call x2, Pallas kernels: 44.2 us -> 19.6 us  [the longest x1 18.6 us: body(): pl.pallas_call(functools.partial(kernel, nz, ny), out_shape=(kept, kept,...]
where the time goes in v5:
time: 20.3 us; the launch traced here: 20.2 us
  Pallas kernels  19.6 us (97%)
  between operations  0.64 us (3%)
    pallas_call x1, Pallas kernels, body(): pl.pallas_call(functools.partial(kernel, nz, ny), out_shape=(kept, kept,...  18.6 us
    pallas_call x1, Pallas kernels, body(): pl.pallas_call(deliver, out_shape=(out, out, out), in_specs=[vmem] * 3, o...  0.97 us

profile of v5, /device:TPU:9, one launch (start us, length us, event | category | flops | bytes accessed | tf_op | source)
XLA Modules:
  0.0 20.2 jit_solution(16018563609587954791)
XLA Ops:
  0.6 18.6 %shard_map.76 = (f32[8,16,512]{2,1,0:T(8,128)S(1)}, f32[8,16,512]{2,1,0:T(8,128)S(1)}, f32[8,16,512]{2,1,0:T(8,128)S(1)}) custom-call(f32[8,16,512]{2,1,0:T(8,128)} %p_in.1, f32[8,16,512]{2,1,0:T(8,128)} %u_in.1, f32[8,16,512]{2,1,0:T(8,128)} %k_in.1, f32[8,16,512]{2,1,0:T(8,128)} %ps_in.1, f32[8,16,512]{2,1,0:T(8,128)} %ts_in.1), custom_call_target="tpu_custom_call" | custom-call | tf_op jit(solution)/shard_map/pallas_call | solution.py:672
  19.2 1.0 %shard_map.77 = (f32[8,16,512]{2,1,0:T(8,128)}, f32[8,16,512]{2,1,0:T(8,128)}, f32[8,16,512]{2,1,0:T(8,128)}) custom-call(f32[8,16,512]{2,1,0:T(8,128)S(1)} %get-tuple-element.6.refs_0_, f32[8,16,512]{2,1,0:T(8,128)S(1)} %get-tuple-element.7.refs_1_, f32[8,16,512]{2,1,0:T(8,128)S(1)} %get-tuple-element.8.refs_2_), custom_call_target="tpu_custom_call" | custom-call | tf_op jit(solution)/shard_map/pallas_call | solution.py:682

commit v6 on v5

--- a/solution.py
+++ b/solution.py
@@ -90,7 +90,7 @@
     p0, p1, d1, d0, u0, t1, t0, u1, kb, sb,
     jz, jxy, gz, gxy,
     r0, rp0, ru0, r1, rp1, ru1, tl1, gr0, pb0,
-    ring_j, ring_g,
+    ring_j, ring_g, held,
     sy0, ry0, sy1, ry1, sy2, ry2, sy3, ry3,
     sc0, rc0, sc1, rc1, sc2, rc2, sc3, rc3,
     ssem, rsem, lsem,
@@ -384,6 +384,46 @@
                 for j in range(C):
                     store(gxy, ring, t, j, out[t][j])
 
+    def hold_layer(zc, p_rows):
+        _, dz, dy, dx = diffs(p0, zc, *p_rows)
+        for t in range(T):
+            for j in range(C):
+                a = (dz[t][j], dy[t][j], dx[t][j])
+                b = basis(*a)
+                for i, value in enumerate((*a, b[3], b[4], b[7], 3.0 * b[8])):
+                    held[i, zc - 1, pl.ds(8 * t, 8), block(j)] = value
+
+    def held_layer(zc, d_rows, z=None):
+        e, ez, ey, ex = diffs(d0, zc, *d_rows)
+        hx, hy = blank(), blank()
+        for t in range(T):
+            for j in range(C):
+                dz, dy, dx, r, qs, big_a, big_b3 = (
+                    held[i, zc - 1, pl.ds(8 * t, 8), block(j)] for i in range(7)
+                )
+                v = (ez[t][j], ey[t][j], ex[t][j])
+                zz, yy, xx = dz * dz, dy * dy, dx * dx
+                q = qs * r
+                mz, my, mx = dz * v[0], dy * v[1], dx * v[2]
+                g = mz + my + mx
+                m = zz * mz + yy * my + xx * mx
+                dq = (4.0 * r * r) * (m - qs * g)
+                k = (
+                    big_a, big_b3, (SLOPE_0 + SLOPE_1 * q) * dq,
+                    r * (TWIST * RISE * dq - (2.0 / 3.0) * big_b3 * g),
+                )
+                store(gz, zc - 1, t, j, turn(dz, zz, v[0], k))
+                if z is not None:
+                    hy[t][j] = turn(dy, yy, v[1], k)
+                    hx[t][j] = turn(dx, xx, v[2], k)
+        if z is None:
+            return
+        c = layer(p0, zc)
+        out = cross(hx, hy, [end_tangent(end_basis(ends(a)), ends(b)) for a, b in zip(c, e)])
+        for t in range(T):
+            for j in range(C):
+                store(gxy, z, t, j, out[t][j])
+
     def flux_ring(p_args, d_args=None, with_flux=True):
         for s in (0, 1):
             dz, dy, dx = ring_diffs(*p_args, s)
@@ -612,16 +652,22 @@
     mobility = with_divergence(jz, jxy, ring_j, mobility_cell)
     over(0, Z, mobility)
 
+    def hold(z):
+        hold_layer(z + 2, halo_rows(ry0, 0, z))
+    over(0, Z, hold, 2)
+    hold_layer(1, corner_rows(rc0, 0, True))
+    hold_layer(Z + 2, corner_rows(rc0, 0, False))
+
     def adjoint0(z):
-        flux_layer(p0, z + 2, halo_rows(ry0, 0, z), d0, halo_rows(ry3, 0, z), False, ring=z)
+        held_layer(z + 2, halo_rows(ry3, 0, z), z)
     arrive(m_y3)
     inner(adjoint0)
     arrive(m_f3 + m_c3)
     flux_ring((ry0, 0, sy0, 0, rc0, 0), (ry3, 0, sy3, 0, rc3, 0), False)
     arrive(m_d0 + m_t0)
     outer(adjoint0)
-    flux_layer(p0, 1, corner_rows(rc0, 0, True), d0, corner_rows(rc3, 0, True), False)
-    flux_layer(p0, Z + 2, corner_rows(rc0, 0, False), d0, corner_rows(rc3, 0, False), False)
+    held_layer(1, corner_rows(rc3, 0, True))
+    held_layer(Z + 2, corner_rows(rc3, 0, False))
 
     def finish(z):
         new_t = laplacian(t0, z + 1, *halo_rows(ry3, 2, z))
@@ -660,7 +706,7 @@
     scratch = [buf(*thick)] * 4 + [buf(*thin)] * 3 + [buf(*flat)] * 3
     scratch += [buf(*thin), buf(*flat)] * 2
     scratch += [buf(*flat)] * 9
-    scratch += [buf(2, Z, X)] * 2
+    scratch += [buf(2, Z, X)] * 2 + [buf(7, *thin)]
     scratch += [buf(2, n, Z, X) for n in (2, 2, 4, 4, 2, 2, 3, 3)]
     scratch += [buf(4, 1, 1, X)] * 8
     count = 48

time: 20.3 us -> 20.2 us (level)
  no operation moved by 1% of the time
where the time goes in v6:
time: 20.2 us; the launch traced here: 20 us
  Pallas kernels  19.4 us (96%)
  between operations  0.64 us (3%)
    pallas_call x1, Pallas kernels, body(): pl.pallas_call(functools.partial(kernel, nz, ny), out_shape=(kept, kept,...  18.4 us
    pallas_call x1, Pallas kernels, body(): pl.pallas_call(deliver, out_shape=(out, out, out), in_specs=[vmem] * 3, o...  0.97 us

profile of v6, /device:TPU:9, one launch (start us, length us, event | category | flops | bytes accessed | tf_op | source)
XLA Modules:
  0.0 20.0 jit_solution(16432488074635088467)
XLA Ops:
  0.6 18.4 %shard_map.76 = (f32[8,16,512]{2,1,0:T(8,128)S(1)}, f32[8,16,512]{2,1,0:T(8,128)S(1)}, f32[8,16,512]{2,1,0:T(8,128)S(1)}) custom-call(f32[8,16,512]{2,1,0:T(8,128)} %p_in.1, f32[8,16,512]{2,1,0:T(8,128)} %u_in.1, f32[8,16,512]{2,1,0:T(8,128)} %k_in.1, f32[8,16,512]{2,1,0:T(8,128)} %ps_in.1, f32[8,16,512]{2,1,0:T(8,128)} %ts_in.1), custom_call_target="tpu_custom_call" | custom-call | tf_op jit(solution)/shard_map/pallas_call | solution.py:718
  19.1 1.0 %shard_map.77 = (f32[8,16,512]{2,1,0:T(8,128)}, f32[8,16,512]{2,1,0:T(8,128)}, f32[8,16,512]{2,1,0:T(8,128)}) custom-call(f32[8,16,512]{2,1,0:T(8,128)S(1)} %get-tuple-element.6.refs_0_, f32[8,16,512]{2,1,0:T(8,128)S(1)} %get-tuple-element.7.refs_1_, f32[8,16,512]{2,1,0:T(8,128)S(1)} %get-tuple-element.8.refs_2_), custom_call_target="tpu_custom_call" | custom-call | tf_op jit(solution)/shard_map/pallas_call | solution.py:728
